TPU v7x, 512 devices: a whole 4x8x8 slice. The times are simulated.
512 devices in a mesh: site: 64 (over y, x, core), term: 8 (over z).
Axes of the slice: x: 4, y: 8, z: 8, core: 2. Of those that a mesh axis runs over, the one named last changes fastest.
Arguments:
- left_env: float32 [64, 16, 8, 128, 128], P('site', 'term'), may hold values from -0.5 to 0.5
- right_env: float32 [64, 16, 8, 128, 128], P('site', 'term'), may hold values from -0.5 to 0.5
- transfer: float32 [64, 8, 128, 128], P('site'), may hold values from -1 to 2, as said below
- psi_start: float32 [64, 8, 128, 128], P('site'), may hold values from -6 to 6
- kept: int32 [64, 8], P('site'), may hold values from 64 to 128
Outputs:
- psi_out: float32 [64, 8, 128, 128], P('site')
- incoming_env: float32 [64, 16, 8, 128, 128], P('site', 'term')
Inputs may be any that keep to these rules, and one draw needn't show every extreme that they name: `transfer`: the identity plus independent entries of deviation 0.2 / sqrt(128).
All inputs are finite; a program needn't handle non-finite values.
Results may differ from a plain program's by a relative error of at most 0.0003.
Values sent between devices are 32-bit elements; how exact they have to be, the bound alone decides.
No kernel may reach another device: no remote copies, remote signals or barrier semaphores. Data moves between devices by JAX's collectives and lax.ppermute only.
A program may use at most 128 MiB of HBM per device.

v0:
```python
import jax
import jax.numpy as jnp
from jax import lax
from jax.sharding import PartitionSpec as P

ITERS = 4


highest = lax.Precision.HIGHEST
norm_eps = 1e-06
step_size = 0.5


def carried_in(value, axis, join, neutral):
    count, mine = (lax.axis_size(axis), lax.axis_index(axis))
    pieces = lax.all_gather(value, axis)
    total = jnp.full_like(value, 0) + jnp.asarray(neutral, value.dtype)

    def hop(position, total):
        longer = join(total, pieces[position])
        return jnp.where(position < mine, longer, total)

    return lax.fori_loop(0, count - 1, hop, total)


def shifted(value, axis, steps):
    count = lax.axis_size(axis)
    leading, last = (max(0, -steps), min(count, count - steps))
    return lax.ppermute(value, axis, [(source, source + steps) for source in range(leading, last)])


def compose(earlier, later):
    return jnp.einsum("sij,sjk->sik", earlier, later, precision=highest)


def apply_terms(left_used, right_part, vector):
    partial_image = jnp.einsum("tsij,sjk->tsik", left_used, vector, precision=highest)
    return jnp.einsum("tsik,tskl->sil", partial_image, right_part, precision=highest)


def per_device(left_env, right_env, transfer, psi_start, kept):
    sectors = transfer.shape[1]
    block = transfer.shape[2]
    identity_block = jnp.broadcast_to(jnp.eye(block, dtype=jnp.float32), (sectors, block, block))
    prefix = carried_in(transfer[0], "site", compose, identity_block)
    left_used = jnp.einsum("sji,tsjk->tsik", prefix, left_env[0], precision=highest)
    left_used = jnp.einsum("tsik,skl->tsil", left_used, prefix, precision=highest)
    right_part = right_env[0]
    start = psi_start[0]
    vector = start / jnp.sqrt(jnp.sum(start * start) + norm_eps)
    for step in range(ITERS):
        image = lax.psum(apply_terms(left_used, right_part, vector), "term")
        energy = jnp.sum(vector * image)
        scale = jnp.sqrt(jnp.sum(image * image) + norm_eps)
        update = vector - step_size * (image - energy * vector) / scale
        vector = update / jnp.sqrt(jnp.sum(update * update) + norm_eps)
    columns = lax.broadcasted_iota(jnp.int32, vector.shape, 2)
    masked = jnp.where(columns < kept[0][:, None, None], vector, jnp.float32(0.0))
    result = masked / jnp.sqrt(jnp.sum(masked * masked) + norm_eps)
    boundary = jnp.einsum("sji,tsjk->tsik", result, left_used, precision=highest)
    boundary = jnp.einsum("tsik,skl->tsil", boundary, result, precision=highest)
    incoming = shifted(boundary[None], "site", 1)
    return (result[None], incoming)


def solution(mesh):
    placed = (
        P("site", "term", None, None, None),
        P("site", "term", None, None, None),
        P("site", None, None, None),
        P("site", None, None, None),
        P("site", None),
    )
    return jax.shard_map(
        per_device,
        mesh=mesh,
        in_specs=placed,
        out_specs=(P("site", None, None, None), P("site", "term", None, None, None)),
        check_vma=False,
    )
```

profile of v0, /device:TPU:32, one launch (start us, length us, event | category | flops | bytes accessed | tf_op | source)
XLA Modules:
  0.0 682.8 jit_solution(392121357070368040)
XLA Ops:
  10.6 150.5 %all-gather.2.cloned.1.call-done = f32[64,8,128,128]{3,2,1,0:T(8,128)} async-done(((f32[1,8,128,128]{3,2,1,0:T(8,128)}), f32[64,8,128,128]{3,2,1,0:T(8,128)}) %all-gather.2.cloned.1.call-update) | async-done | bytes 33554448 | tf_op jit(solution)/shard_map/all_gather | solution.py:16
  161.0 134.5 %while.13 = (s32[]{:T(128)}, f32[8,128,128]{1,2,0:T(8,128)S(1)}, s32[]{:T(128)}, f32[64,8,128,128]{3,2,1,0:T(8,128)}, s32[]{:T(128)}) while((s32[]{:T(128)}, f32[8,128,128]{1,2,0:T(8,128)S(1)}, s32[]{:T(128)}, f32[64,8,128,128]{3,2,1,0:T(8,128)}, s32[]{:T(128)}) %tuple.43), condition=%wide.region_2.3_spmd, body=%wide.region_1.2_spmd.sunk | while | flops 201457664 | bytes 3146311 | solution.py:23
  163.2 2.1 fusion.45
  169.6 2.1 fusion.45
  171.8 2.1 fusion.45
  173.9 2.1 fusion.45
  176.1 2.1 fusion.45
  184.6 2.1 fusion.45
  186.7 2.1 fusion.45
  188.9 2.1 fusion.45
  197.4 2.1 fusion.45
  199.5 2.1 fusion.45
  201.7 2.1 fusion.45
  203.8 2.1 fusion.45
  210.2 2.1 fusion.45
  212.3 2.1 fusion.45
  214.5 2.1 fusion.45
  216.6 2.1 fusion.45
  225.2 2.1 fusion.45
  227.3 2.1 fusion.45
  229.4 2.1 fusion.45
  238.0 2.1 fusion.45
  240.1 2.1 fusion.45
  242.2 2.1 fusion.45
  244.4 2.1 fusion.45
  250.8 2.1 fusion.45
  252.9 2.1 fusion.45
  255.0 2.1 fusion.45
  257.2 2.1 fusion.45
  265.7 2.1 fusion.45
  267.8 2.1 fusion.45
  270.0 2.1 fusion.45
  278.5 2.1 fusion.45
  280.7 2.1 fusion.45
  282.8 2.1 fusion.45
  284.9 2.1 fusion.45
  291.3 2.1 fusion.45
  295.5 2.2 convolution_bitcast_fusion.8
  298.8 3.0 convolution_bitcast_fusion.6
  303.9 79.6 %all-reduce.5.cloned.1.call-done = f32[8,128,128]{2,1,0:T(8,128)} async-done(((f32[8,128,128]{2,1,0:T(8,128)}), f32[8,128,128]{2,1,0:T(8,128)}) %all-reduce.5.cloned.1.call-update) | async-done | bytes 524304 | tf_op jit(solution)/shard_map/psum | solution.py:52
  386.1 2.6 multiply_reduce_fusion.10
  393.6 77.6 %all-reduce.7.cloned.1.call-done = f32[8,128,128]{2,1,0:T(8,128)} async-done(((f32[8,128,128]{2,1,0:T(8,128)}), f32[8,128,128]{2,1,0:T(8,128)}) %all-reduce.7.cloned.1.call-update) | async-done | bytes 524304 | tf_op jit(solution)/shard_map/psum | solution.py:52
  473.7 2.4 multiply_reduce_fusion.7
  480.8 77.8 %all-reduce.9.cloned.1.call-done = f32[8,128,128]{2,1,0:T(8,128)} async-done(((f32[8,128,128]{2,1,0:T(8,128)}), f32[8,128,128]{2,1,0:T(8,128)}) %all-reduce.9.cloned.1.call-update) | async-done | bytes 524304 | tf_op jit(solution)/shard_map/psum | solution.py:52
  561.1 2.4 multiply_reduce_fusion.4
  568.2 77.9 %all-reduce.11.cloned.1.call-done = f32[8,128,128]{2,1,0:T(8,128)} async-done(((f32[8,128,128]{2,1,0:T(8,128)}), f32[8,128,128]{2,1,0:T(8,128)}) %all-reduce.11.cloned.1.call-update) | async-done | bytes 524304 | tf_op jit(solution)/shard_map/psum | solution.py:52
  648.6 2.4 multiply_reduce_fusion.1
  658.3 16.6 %collective-permute-done = f32[1,2,8,128,128]{3,4,1,2,0:T(8,128)S(1)} collective-permute-done((f32[1,2,8,128,128]{3,4,1,2,0:T(8,128)S(1)}, f32[1,2,8,128,128]{3,4,1,2,0:T(8,128)S(1)}, u32[]{:S(2)}, u32[]{:S(2)}) %collective-permute-start) | collective-permute-done | bytes 1048608 | tf_op jit(solution)/shard_map/ppermute | solution.py:29
  (126 shorter events, 92.3 us)
Async XLA Ops:
  7.2 294.7 %copy-start = (f32[1,2,8,128,128]{4,3,2,1,0:T(8,128)S(1)}, f32[1,2,8,128,128]{4,3,2,1,0:T(8,128)}, u32[]{:S(2)}) copy-start(f32[1,2,8,128,128]{4,3,2,1,0:T(8,128)} %param.8) | copy-start | bytes 3145732
  7.2 644.5 %copy-start.1 = (s32[1,8]{1,0:T(1,128)S(1)}, s32[1,8]{1,0:T(1,128)}, u32[]{:S(2)}) copy-start(s32[1,8]{1,0:T(1,128)} %param.11) | copy-start | bytes 100
  7.2 153.8 %all-gather.2.cloned.1.call-start = ((), (), s32[]{:S(2)}) async-start(), calls=%async_computation | async-start | bytes 34078720 | tf_op jit(solution)/shard_map/all_gather | solution.py:16
  7.9 375.6 %all-reduce.5.cloned.1.call-start = ((), (), s32[]{:S(2)}) async-start(), calls=%async_computation.1 | async-start | bytes 1048576 | tf_op jit(solution)/shard_map/psum | solution.py:52
  303.8 167.4 %all-reduce.7.cloned.1.call-start = ((), (), s32[]{:S(2)}) async-start(), calls=%async_computation.2 | async-start | bytes 1048576 | tf_op jit(solution)/shard_map/psum | solution.py:52
  393.4 165.3 %all-reduce.9.cloned.1.call-start = ((), (), s32[]{:S(2)}) async-start(), calls=%async_computation.3 | async-start | bytes 1048576 | tf_op jit(solution)/shard_map/psum | solution.py:52
  480.8 165.3 %all-reduce.11.cloned.1.call-start = ((), (), s32[]{:S(2)}) async-start(), calls=%async_computation.4 | async-start | bytes 1048576 | tf_op jit(solution)/shard_map/psum | solution.py:52
  655.5 19.4 %collective-permute-start = (f32[1,2,8,128,128]{3,4,1,2,0:T(8,128)S(1)}, f32[1,2,8,128,128]{3,4,1,2,0:T(8,128)S(1)}, u32[]{:S(2)}, u32[]{:S(2)}) collective-permute-start(f32[1,2,8,128,128]{3,4,1,2,0:T(8,128)S(1)} %convolution_bitcast_fusion.1), channel_id=1, source_target_pairs={{0,8},{8,16},{16,24},{24,32},{32,40},{40,48},{48,56},{56,64},{64,7... | collective-permute-start | bytes 3145736 | tf_op jit(solution)/shard_map/ppermute | solution.py:29
Sparse Core Ops, SparseCore 0:
  11.4 149.5 all-gather.1
  303.9 79.5 all-reduce.4
  393.5 77.7 all-reduce.6
  480.9 77.6 all-reduce.8
  568.3 77.7 all-reduce.10
where the time goes:
time: 686 us; the launch traced here: 683 us
  waiting for transfers between devices  481 us (70%)
  matrix products  152 us (22%)
  between operations  20.9 us (3%)
  other arithmetic  20.8 us (3%)
    psum x4, waiting for transfers between devices, per_device(): image = lax.psum(apply_terms(left_used, right_part, vector), 'term')  313 us
    all_gather x1, waiting for transfers between devices, carried_in(): pieces = lax.all_gather(value, axis)  150 us
    dot_general x63, matrix products, compose(): return jnp.einsum('sij,sjk->sik', earlier, later, precision=highest)  130 us
    ppermute x1, waiting for transfers between devices, shifted(): lax.ppermute(value, axis, [(source, source + steps) for source in range(l...  16.6 us
  transfers between devices with their start and end apart: 6, of which 6 were waited for; matrix products, arithmetic and copies ran while one was open for 0% of the time, Pallas kernels for 0%

commit v1 on v0

v1 whole, which is shorter than its diff:
```python
import functools

import jax
import jax.numpy as jnp
from jax import lax
from jax.experimental import pallas as pl
from jax.experimental.pallas import tpu as pltpu
from jax.sharding import Mesh, PartitionSpec as P

ITERS = 4
norm_eps = 1e-06
step_size = 0.5
SITE = ("y2", "y1", "y0", "x1", "x0", "c")
SCAN = ("c", "x0", "x1", "y0", "y1", "y2")
TERM = "z"
VMEM_LIMIT = 48 * 1024 * 1024


def halves(x):
    high = x.astype(jnp.bfloat16)
    low = (x - high.astype(jnp.float32)).astype(jnp.bfloat16)
    return high, low


def mm(a, b):
    return jnp.dot(a, b, preferred_element_type=jnp.float32)


def left_operand(a):
    return jnp.concatenate(halves(a), axis=1)


def right_operand(b):
    high, low = halves(b)
    top = jnp.concatenate([high, low], axis=1)
    bottom = jnp.concatenate([high, jnp.zeros_like(high)], axis=1)
    return jnp.concatenate([top, bottom], axis=0)


def joined(a, b):
    both = mm(a, right_operand(b))
    size = b.shape[1]
    return both[:, :size] + both[:, size:]


def total(x):
    return jnp.sum(jnp.sum(x, axis=0, keepdims=True), axis=1, keepdims=True)


def krylov_kernel(z_ref, blocks_ref, prefix_ref, start_ref, basis_ref, sent_ref, left_ref, right_ref):
    groups, per_group, size, _ = blocks_ref.shape
    own = per_group // 2
    terms = groups * own
    for group in range(groups):
        for term in range(own):
            at = (group * own + term) * size
            left_ref[at:at + size, :] = left_operand(blocks_ref[group, term])
            high, low = halves(blocks_ref[group, own + term])
            right_ref[at:at + size, :] = jnp.concatenate([high, low], axis=1)
    prefix = prefix_ref[...]
    forward = left_operand(prefix)
    backward = left_operand(prefix.T)
    squares = jnp.zeros((size, size), jnp.float32)
    for sector in range(start_ref.shape[0]):
        squares = squares + start_ref[sector] * start_ref[sector]
    x = start_ref[z_ref[0]] / jnp.sqrt(total(squares) + norm_eps)
    basis_ref[0] = x
    lane = lax.broadcasted_iota(jnp.int32, (1, size), 1)
    row = jnp.zeros((1, size), jnp.float32)
    basis = [x]
    for step in range(ITERS):
        w = joined(forward, x)
        middle = joined(left_ref[...], w)
        high, low = halves(middle)
        wide = jnp.concatenate(
            [
                jnp.concatenate([part[t * size:(t + 1) * size] for t in range(terms)], axis=1)
                for part in (high, low)
            ],
            axis=0,
        )
        both = mm(wide, right_ref[...])
        y = both[:size, :size] + (both[:size, size:] + both[size:, :size])
        y = joined(backward, y)
        length = jnp.sqrt(total(y * y))
        x = y / jnp.maximum(length, 1e-30)
        basis_ref[step + 1] = x
        basis.append(x)
        row = row + jnp.where(lane == step, length, 0.0)
    place = ITERS
    for i in range(ITERS + 1):
        for j in range(i, ITERS + 1):
            row = row + jnp.where(lane == place, total(basis[i] * basis[j]), 0.0)
            place += 1
    sheet = jnp.broadcast_to(row, (8, size))
    for target in range(groups):
        sent_ref[target, :size, :] = prefix
        sent_ref[target, size:, :] = sheet


def combine_kernel(z_ref, kept_ref, scalars_ref, basis_ref, sent_ref):
    table = scalars_ref[:, 0, :]
    sectors, size = table.shape

    def item(index):
        return table[:, index:index + 1]

    def over(x):
        return jnp.sum(x, axis=0, keepdims=True)

    rates = [jnp.ones((sectors, 1), jnp.float32)]
    ratio = []
    for j in range(ITERS):
        longer = rates[j] * item(j)
        largest = jnp.maximum(jnp.max(longer, axis=0, keepdims=True), 1e-30)
        ratio.append(largest)
        rates.append(longer / largest)
    gram = {}
    place = ITERS
    for i in range(ITERS + 1):
        for j in range(i, ITERS + 1):
            gram[i, j] = gram[j, i] = over(rates[i] * rates[j] * item(place))
            place += 1
    zero = jnp.zeros((1, 1), jnp.float32)
    vector = [jnp.ones((1, 1), jnp.float32)] + [zero] * ITERS

    def inner(a, b, upto_a, upto_b):
        out = zero
        for i in range(upto_a[0], upto_a[1] + 1):
            for j in range(upto_b[0], upto_b[1] + 1):
                out = out + a[i] * b[j] * gram[i, j]
        return out

    for step in range(ITERS):
        image = [zero] + [vector[j] * ratio[j] for j in range(ITERS)]
        energy = inner(vector, image, (0, step), (1, step + 1))
        scale = jnp.sqrt(inner(image, image, (1, step + 1), (1, step + 1)) + norm_eps)
        update = [vector[j] - step_size * (image[j] - energy * vector[j]) / scale for j in range(ITERS + 1)]
        length = jnp.sqrt(inner(update, update, (0, step + 1), (0, step + 1)) + norm_eps)
        vector = [part / length for part in update]

    mine = lax.broadcasted_iota(jnp.int32, (sectors, 1), 0) == z_ref[0]
    result = jnp.zeros((size, size), jnp.float32)
    for j in range(ITERS + 1):
        factor = over(jnp.where(mine, rates[j], 0.0)) * vector[j]
        result = result + factor * basis_ref[j]
    columns = lax.broadcasted_iota(jnp.int32, (size, size), 1)
    result = jnp.where(columns < kept_ref[0, z_ref[0]], result, 0.0)
    for target in range(sectors):
        sent_ref[target] = result


def finish_kernel(vector_ref, prefix_ref, psi_ref, moved_ref):
    sectors, size, _ = vector_ref.shape
    squares = jnp.zeros((size, size), jnp.float32)
    for sector in range(sectors):
        squares = squares + vector_ref[sector] * vector_ref[sector]
    length = jnp.sqrt(total(squares) + norm_eps)
    for sector in range(sectors):
        psi = vector_ref[sector] / length
        psi_ref[0, sector] = psi
        moved_ref[sector] = joined(left_operand(prefix_ref[sector, :size, :]), psi)


def boundary_kernel(moved_ref, left_ref, out_ref):
    own, sectors, size, _ = left_ref.shape
    for sector in range(sectors):
        u = moved_ref[sector]
        right = right_operand(u)
        across = left_operand(u.T)
        for term in range(own):
            half = mm(left_operand(left_ref[term, sector]), right)
            half = half[:, :size] + half[:, size:]
            out_ref[0, term, sector] = joined(across, half)


def vmem():
    return pl.BlockSpec(memory_space=pltpu.VMEM)


def smem():
    return pl.BlockSpec(memory_space=pltpu.SMEM)


def call(kernel, out_shape, in_specs, flops, scratch=()):
    return pl.pallas_call(
        kernel,
        out_shape=out_shape,
        in_specs=in_specs,
        out_specs=jax.tree.map(lambda _: vmem(), out_shape),
        scratch_shapes=scratch,
        compiler_params=pltpu.CompilerParams(vmem_limit_bytes=VMEM_LIMIT),
        cost_estimate=pl.CostEstimate(flops=flops, bytes_accessed=4 << 20, transcendentals=0),
    )


def struct(*shape):
    return jax.ShapeDtypeStruct(shape, jnp.float32)


def product(a, b):
    return jnp.dot(a, b, precision=lax.Precision.HIGHEST, preferred_element_type=jnp.float32)


def scanned(own):
    whole = own
    prefix = None
    for level, axis in enumerate(SCAN):
        with jax.named_scope("scan_" + axis):
            pair = lax.all_gather(whole, axis)
            upper = lax.axis_index(axis) == 1
            if prefix is None:
                prefix = jnp.where(upper, pair[0], jnp.eye(own.shape[0], dtype=own.dtype))
            else:
                prefix = jnp.where(upper, product(pair[0], prefix), prefix)
            if level + 1 < len(SCAN):
                whole = product(pair[0], pair[1])
    return prefix


def per_device(left_env, right_env, transfer, psi_start, kept):
    left, right, transfer, psi = left_env[0], right_env[0], transfer[0], psi_start[0]
    own, sectors, size, _ = left.shape
    z = lax.axis_index(TERM)
    spot = z[None]
    with jax.named_scope("gather_terms"):
        outgoing = jnp.concatenate([left, right], axis=0)
        blocks = lax.all_to_all(outgoing, TERM, 1, 0, tiled=False)
    with jax.named_scope("prefix"):
        prefix = scanned(lax.dynamic_index_in_dim(transfer, z, 0, keepdims=False))
    pairs = [(source, source + 1) for source in range(63)]
    with jax.named_scope("left_previous"):
        late, _ = lax.optimization_barrier((left, prefix))
        left_previous = lax.ppermute(late, SITE, pairs)
    with jax.named_scope("krylov"):
        terms = own * sectors
        basis, sent = call(
            krylov_kernel,
            (struct(ITERS + 1, size, size), struct(sectors, size + 8, size)),
            [smem(), vmem(), vmem(), vmem()],
            ITERS * terms * 4 * 2 * 3 * size**3,
            [pltpu.VMEM((terms * size, 2 * size), jnp.bfloat16)] * 2,
        )(spot, blocks, prefix, psi)
    with jax.named_scope("share_scalars"):
        shared = lax.all_to_all(sent, TERM, 0, 0, tiled=True)
    with jax.named_scope("combine"):
        scalars = shared[:, size:, :]
        sent = call(
            combine_kernel,
            struct(sectors, size, size),
            [smem(), smem(), vmem(), vmem()],
            size**2 * 100,
        )(spot, kept, scalars, basis)
    with jax.named_scope("share_psi"):
        vector = lax.all_to_all(sent, TERM, 0, 0, tiled=True)
    with jax.named_scope("finish"):
        result, moved = call(
            finish_kernel,
            (struct(1, sectors, size, size), struct(sectors, size, size)),
            [vmem(), vmem()],
            sectors * 6 * size**3,
        )(vector, shared)
    with jax.named_scope("hand_on"):
        moved = lax.ppermute(moved, SITE, pairs)
    with jax.named_scope("boundary"):
        incoming = call(
            boundary_kernel,
            struct(1, own, sectors, size, size),
            [vmem(), vmem()],
            own * sectors * 12 * size**3,
        )(moved, left_previous)
    return result, incoming


def solution(mesh):
    fine = Mesh(mesh.devices.reshape((2,) * 6 + (8,)), SITE + (TERM,))
    placed = (
        P(SITE, TERM, None, None, None),
        P(SITE, TERM, None, None, None),
        P(SITE, None, None, None),
        P(SITE, None, None, None),
        P(SITE, None),
    )
    return jax.shard_map(
        per_device,
        mesh=fine,
        in_specs=placed,
        out_specs=(P(SITE, None, None, None), P(SITE, TERM, None, None, None)),
        check_vma=False,
    )
```

time: 686 us -> 128 us (0.19)
  waiting for transfers between devices: 481 us -> 39.8 us
  matrix products: 152 us -> 2.05 us
  blocking collectives: 0 us -> 53.9 us
  between operations: 20.9 us -> 0.79 us
  other arithmetic: 20.8 us -> 1.74 us
  starting transfers between devices: 2.3 us -> 17.6 us
  Pallas kernels: 0 us -> 10.1 us
    psum x4 -> x0, waiting for transfers between devices: 313 us -> none  [per_device(): image = lax.psum(apply_terms(left_used, right_part, vector), 'term')]
    all_gather x1 -> x0, waiting for transfers between devices: 150 us -> none  [carried_in(): pieces = lax.all_gather(value, axis)]
    dot_general x75 -> x10, matrix products: 152 us -> 2.05 us  [product(): jnp.dot(a, b, precision=lax.Precision.HIGHEST, preferred_element_type=jnp...]
    all_gather x0 -> x6, blocking collectives: none -> 34.1 us  [scanned(): pair = lax.all_gather(whole, axis)]
    all_to_all x0 -> x2, waiting for transfers between devices: none -> 27.9 us  [the longest x1 15 us: per_device(): blocks = lax.all_to_all(outgoing, TERM, 1, 0, tiled=False)]
    reduce_sum x10 -> x0, other arithmetic: 19.9 us -> none  [the longest x4 9.94 us: per_device(): vector = update / jnp.sqrt(jnp.sum(update * update) + norm_eps)]
    all_to_all x0 -> x1, blocking collectives: none -> 19.8 us  [per_device(): shared = lax.all_to_all(sent, TERM, 0, 0, tiled=True)]
    all_to_all x0 -> x2, starting transfers between devices: none -> 13.8 us  [the longest x1 10.3 us: per_device(): blocks = lax.all_to_all(outgoing, TERM, 1, 0, tiled=False)]
  transfers between devices with their start and end apart: 6 -> 4, of which waited for: 6 -> 4; matrix products, arithmetic and copies ran while one was open for 0% -> 2% of each run, Pallas kernels for 0% -> 1%
where the time goes in v1:
time: 128 us
  blocking collectives  53.9 us (42%)
  waiting for transfers between devices  39.8 us (31%)
  starting transfers between devices  17.6 us (14%)
  Pallas kernels  10.1 us (8%)
  matrix products  2.05 us (2%)
  other arithmetic  1.74 us (1%)
  local copies, waits for them, and re-layouts  1.52 us (1%)
    all_gather x6, blocking collectives, scanned(): pair = lax.all_gather(whole, axis)  34.1 us
    all_to_all x1, blocking collectives, per_device(): shared = lax.all_to_all(sent, TERM, 0, 0, tiled=True)  19.8 us
    all_to_all x1, waiting for transfers between devices, per_device(): blocks = lax.all_to_all(outgoing, TERM, 1, 0, tiled=False)  15 us
    all_to_all x1, waiting for transfers between devices, per_device(): vector = lax.all_to_all(sent, TERM, 0, 0, tiled=True)  12.9 us
    all_to_all x1, starting transfers between devices, per_device(): blocks = lax.all_to_all(outgoing, TERM, 1, 0, tiled=False)  10.3 us
    ppermute x1, waiting for transfers between devices, per_device(): moved = lax.ppermute(moved, SITE, pairs)  10.1 us
    pallas_call x1, Pallas kernels, per_device(): call(krylov_kernel, (struct(ITERS + 1, size, size), struct(sectors, size...  5.43 us
    all_to_all x1, starting transfers between devices, per_device(): vector = lax.all_to_all(sent, TERM, 0, 0, tiled=True)  3.49 us
  transfers between devices with their start and end apart: 4, of which 4 were waited for; matrix products, arithmetic and copies ran while one was open for 2% of the time, Pallas kernels for 1%

profile of v1, /device:TPU:32, one launch (start us, length us, event | category | flops | bytes accessed | tf_op | source)
XLA Modules:
  0.0 127.5 jit_solution(1070952284275467334)
XLA Ops:
  0.6 0.0 copy-start
  0.6 1.7 %maximum_bitcast_fusion = f32[1,4,8,128,128]{4,3,2,1,0:T(8,128)S(1)} fusion(f32[2,8,128,128]{3,2,1,0:T(8,128)} %bitcast.34, f32[2,8,128,128]{3,2,1,0:T(8,128)} %bitcast.35), kind=kLoop, calls=%fused_computation | loop fusion | flops 524288 | bytes 4194304 | tf_op jit(solution)/shard_map/gather_terms/broadcast_in_dim | solution.py:228
  2.4 1.5 %copy.8 = f32[1,4,8,128,128]{4,3,1,0,2:T(8,128)} copy(f32[1,4,8,128,128]{4,3,2,1,0:T(8,128)S(1)} %maximum_bitcast_fusion) | data formatting | bytes 4194304 | tf_op jit(solution)/shard_map/gather_terms/broadcast_in_dim | solution.py:228
  3.9 10.3 %all-to-all-start = ((f32[1,4,8,128,128]{4,3,1,0,2:T(8,128)}), f32[1,4,8,128,128]{4,3,1,0,2:T(8,128)S(1)}, u32[]{:S(2)}, u32[]{:S(2)}) async-start(f32[1,4,8,128,128]{4,3,1,0,2:T(8,128)} %copy.8), calls=%async_computation | async-start | bytes 4194304 | tf_op jit(solution)/shard_map/gather_terms/all_to_all | solution.py:228
  14.2 0.0 copy-start.2
  14.2 0.0 copy-done
  14.2 2.0 %all-gather = f32[2,1,128,128]{3,2,1,0:T(8,128)S(1)} all-gather(f32[1,1,128,128]{3,2,1,0:T(8,128)S(1)} %constant_dynamic-slice_fusion), channel_id=2, replica_groups=mesh['y2'=2,'y1'=2,'y0'=2,'x1'=2,'x0'=2,'c'=2,'z'=8] {'c'}, dimensions={0}, use_global_device_ids=true | all-gather | bytes 196608 | tf_op jit(solution)/shard_map/prefix/scan_c/all_gather | solution.py:210
  16.3 0.2 fusion.9
  16.5 4.9 %all-gather.1 = f32[256,128]{1,0:T(8,128)S(1)} all-gather(f32[128,128]{1,0:T(8,128)S(1)} %fusion.9), channel_id=3, replica_groups=mesh['y2'=2,'y1'=2,'y0'=2,'x1'=2,'x0'=2,'c'=2,'z'=8] {'x0'}, dimensions={0}, use_global_device_ids=true | all-gather | bytes 196608 | tf_op jit(solution)/shard_map/prefix/scan_x0/all_gather | solution.py:210
  21.4 0.2 fusion.7
  21.6 6.4 %all-gather.2 = f32[256,128]{1,0:T(8,128)S(1)} all-gather(f32[128,128]{1,0:T(8,128)S(1)} %fusion.7), channel_id=4, replica_groups=mesh['y2'=2,'y1'=2,'y0'=2,'x1'=2,'x0'=2,'c'=2,'z'=8] {'x1'}, dimensions={0}, use_global_device_ids=true | all-gather | bytes 196608 | tf_op jit(solution)/shard_map/prefix/scan_x1/all_gather | solution.py:210
  28.1 0.2 fusion.5
  28.3 4.9 %all-gather.3 = f32[256,128]{1,0:T(8,128)S(1)} all-gather(f32[128,128]{1,0:T(8,128)S(1)} %fusion.5), channel_id=5, replica_groups=mesh['y2'=2,'y1'=2,'y0'=2,'x1'=2,'x0'=2,'c'=2,'z'=8] {'y0'}, dimensions={0}, use_global_device_ids=true | all-gather | bytes 196608 | tf_op jit(solution)/shard_map/prefix/scan_y0/all_gather | solution.py:210
  33.2 0.2 fusion.3
  33.4 6.6 %all-gather.4 = f32[256,128]{1,0:T(8,128)S(1)} all-gather(f32[128,128]{1,0:T(8,128)S(1)} %fusion.3), channel_id=6, replica_groups=mesh['y2'=2,'y1'=2,'y0'=2,'x1'=2,'x0'=2,'c'=2,'z'=8] {'y1'}, dimensions={0}, use_global_device_ids=true | all-gather | bytes 196608 | tf_op jit(solution)/shard_map/prefix/scan_y1/all_gather | solution.py:210
  40.1 0.2 fusion.1
  40.3 9.1 %all-gather.5 = f32[256,128]{1,0:T(8,128)S(1)} all-gather(f32[128,128]{1,0:T(8,128)S(1)} %fusion.1), channel_id=7, replica_groups=mesh['y2'=2,'y1'=2,'y0'=2,'x1'=2,'x0'=2,'c'=2,'z'=8] {'y2'}, dimensions={0}, use_global_device_ids=true | all-gather | bytes 196608 | tf_op jit(solution)/shard_map/prefix/scan_y2/all_gather | solution.py:210
  49.4 0.2 convolution_select_fusion.4
  49.6 0.2 convolution_select_fusion.3
  49.8 0.2 convolution_select_fusion.2
  50.0 0.2 convolution_select_fusion.1
  50.2 0.2 convolution_select_fusion.prefix_ref
  50.4 15.0 %all-to-all-done = f32[1,4,8,128,128]{4,3,1,0,2:T(8,128)S(1)} async-done(((f32[1,4,8,128,128]{4,3,1,0,2:T(8,128)}), f32[1,4,8,128,128]{4,3,1,0,2:T(8,128)S(1)}, u32[]{:S(2)}, u32[]{:S(2)}) %all-to-all-start) | async-done | bytes 2097184 | tf_op jit(solution)/shard_map/gather_terms/all_to_all | solution.py:228
  65.4 0.0 copy-done.2
  65.4 0.0 copy-start.1
  65.4 5.4 %krylov.1 = (f32[5,128,128]{2,1,0:T(8,128)S(1)}, f32[8,136,128]{2,1,0:T(8,128)S(1)}) custom-call(s32[1]{0:T(128)} %bitcast.z_ref, f32[8,4,128,128]{3,2,1,0:T(8,128)S(1)} %bitcast.32, f32[128,128]{1,0:T(8,128)S(1)} %convolution_select_fusion.prefix_ref, f32[8,128,128]{2,1,0:T(8,128)S(1)} %bitcast.33), custom_call_target="tpu_custom_call" | custom-call | flops 3221225472 | bytes 4194304 | tf_op jit(solution)/shard_map/krylov/pallas_call | solution.py:237
  70.8 19.8 %all_to_all.25.prefix_ref = f32[8,136,128]{2,1,0:T(8,128)S(1)} all-to-all(f32[8,136,128]{2,1,0:T(8,128)S(1)} %get-tuple-element.7), channel_id=1, replica_groups=mesh['y2'=2,'y1'=2,'y0'=2,'x1'=2,'x0'=2,'c'=2,'z'=8] {'z'}, dimensions={0} | all-to-all | bytes 1114112 | tf_op jit(solution)/shard_map/share_scalars/all_to_all | solution.py:245
  90.7 0.0 copy-done.1
  90.7 1.7 %combine.1 = f32[8,128,128]{2,1,0:T(8,128)} custom-call(s32[1]{0:T(128)} %bitcast.z_ref, s32[1,8]{1,0:T(1,128)S(1)} %copy-done.1, f32[8,8,128]{2,1,0:T(8,128)S(1)} %slice.75.scalars_ref, f32[5,128,128]{2,1,0:T(8,128)S(1)} %get-tuple-element.8.basis_ref), custom_call_target="tpu_custom_call" | custom-call | flops 1638400 | bytes 4194304 | tf_op jit(solution)/shard_map/combine/pallas_call | solution.py:248
  92.4 3.5 %all-to-all-start.2 = ((f32[8,128,128]{2,1,0:T(8,128)}), f32[8,128,128]{2,1,0:T(8,128)S(1)}, u32[]{:S(2)}, u32[]{:S(2)}) async-start(f32[8,128,128]{2,1,0:T(8,128)} %combine.1), calls=%async_computation.2 | async-start | bytes 1048576 | tf_op jit(solution)/shard_map/share_psi/all_to_all | solution.py:255
  95.9 1.9 %collective-permute-start.1 = (f32[2,8,128,128]{3,2,1,0:T(8,128)}, f32[2,8,128,128]{3,2,1,0:T(8,128)S(1)}, u32[]{:S(2)}, u32[]{:S(2)}) collective-permute-start(f32[2,8,128,128]{3,2,1,0:T(8,128)} %bitcast.36), channel_id=1, source_target_pairs={{0,8},{8,16},{16,24},{24,32},{32,40},{40,48},{48,56},{56,64},{64,7... | collective-permute-start | bytes 3145736 | tf_op jit(solution)/shard_map/left_previous/ppermute | solution.py:234
  97.8 12.9 %all-to-all-done.2.vector_ref = f32[8,128,128]{2,1,0:T(8,128)S(1)} async-done(((f32[8,128,128]{2,1,0:T(8,128)}), f32[8,128,128]{2,1,0:T(8,128)S(1)}, u32[]{:S(2)}, u32[]{:S(2)}) %all-to-all-start.2) | async-done | bytes 524320 | tf_op jit(solution)/shard_map/share_psi/all_to_all | solution.py:255
  110.7 1.1 finish.1
  111.9 1.9 %collective-permute-start = (f32[8,128,128]{2,1,0:T(8,128)S(1)}, f32[8,128,128]{2,1,0:T(8,128)S(1)}, u32[]{:S(2)}, u32[]{:S(2)}) collective-permute-start(f32[8,128,128]{2,1,0:T(8,128)S(1)} %get-tuple-element.10), channel_id=1, source_target_pairs={{0,8},{8,16},{16,24},{24,32},{32,40},{40,48},{48,56},{56,64},{64,7... | collective-permute-start | bytes 1572872 | tf_op jit(solution)/shard_map/hand_on/ppermute | solution.py:264
  113.8 1.8 %collective-permute-done.1.left_ref = f32[2,8,128,128]{3,2,1,0:T(8,128)S(1)} collective-permute-done((f32[2,8,128,128]{3,2,1,0:T(8,128)}, f32[2,8,128,128]{3,2,1,0:T(8,128)S(1)}, u32[]{:S(2)}, u32[]{:S(2)}) %collective-permute-start.1) | collective-permute-done | bytes 1048608 | tf_op jit(solution)/shard_map/left_previous/ppermute | solution.py:234
  115.5 10.1 %collective-permute-done.moved_ref = f32[8,128,128]{2,1,0:T(8,128)S(1)} collective-permute-done((f32[8,128,128]{2,1,0:T(8,128)S(1)}, f32[8,128,128]{2,1,0:T(8,128)S(1)}, u32[]{:S(2)}, u32[]{:S(2)}) %collective-permute-start) | collective-permute-done | bytes 524320 | tf_op jit(solution)/shard_map/hand_on/ppermute | solution.py:264
  125.7 1.8 %boundary.1 = f32[1,2,8,128,128]{4,3,2,1,0:T(8,128)} custom-call(f32[8,128,128]{2,1,0:T(8,128)S(1)} %collective-permute-done.moved_ref, f32[2,8,128,128]{3,2,1,0:T(8,128)S(1)} %collective-permute-done.1.left_ref), custom_call_target="tpu_custom_call" | custom-call | flops 402653184 | bytes 4194304 | tf_op jit(solution)/shard_map/boundary/pallas_call | solution.py:266
  (2 shorter events, 0.0 us)
Async XLA Ops:
  0.6 13.6 %copy-start = (f32[1,8,128,128]{3,2,1,0:T(8,128)S(1)}, f32[1,8,128,128]{3,2,1,0:T(8,128)}, u32[]{:S(2)}) copy-start(f32[1,8,128,128]{3,2,1,0:T(8,128)} %param.7) | copy-start | bytes 1572868
  3.9 61.5 %all-to-all-start = ((f32[1,4,8,128,128]{4,3,1,0,2:T(8,128)}), f32[1,4,8,128,128]{4,3,1,0,2:T(8,128)S(1)}, u32[]{:S(2)}, u32[]{:S(2)}) async-start(f32[1,4,8,128,128]{4,3,1,0,2:T(8,128)} %copy.8), calls=%async_computation | async-start | bytes 4194304 | tf_op jit(solution)/shard_map/gather_terms/all_to_all | solution.py:228
  14.2 51.2 %copy-start.2 = (f32[1,8,128,128]{3,2,1,0:T(8,128)S(1)}, f32[1,8,128,128]{3,2,1,0:T(8,128)}, u32[]{:S(2)}) copy-start(f32[1,8,128,128]{3,2,1,0:T(8,128)} %param.8) | copy-start | bytes 1572868
  65.4 25.3 %copy-start.1 = (s32[1,8]{1,0:T(1,128)S(1)}, s32[1,8]{1,0:T(1,128)}, u32[]{:S(2)}) copy-start(s32[1,8]{1,0:T(1,128)} %kept_ref.1) | copy-start | bytes 100
  92.4 18.4 %all-to-all-start.2 = ((f32[8,128,128]{2,1,0:T(8,128)}), f32[8,128,128]{2,1,0:T(8,128)S(1)}, u32[]{:S(2)}, u32[]{:S(2)}) async-start(f32[8,128,128]{2,1,0:T(8,128)} %combine.1), calls=%async_computation.2 | async-start | bytes 1048576 | tf_op jit(solution)/shard_map/share_psi/all_to_all | solution.py:255
  95.9 19.7 %collective-permute-start.1 = (f32[2,8,128,128]{3,2,1,0:T(8,128)}, f32[2,8,128,128]{3,2,1,0:T(8,128)S(1)}, u32[]{:S(2)}, u32[]{:S(2)}) collective-permute-start(f32[2,8,128,128]{3,2,1,0:T(8,128)} %bitcast.36), channel_id=1, source_target_pairs={{0,8},{8,16},{16,24},{24,32},{32,40},{40,48},{48,56},{56,64},{64,7... | collective-permute-start | bytes 3145736 | tf_op jit(solution)/shard_map/left_previous/ppermute | solution.py:234
  111.9 13.8 %collective-permute-start = (f32[8,128,128]{2,1,0:T(8,128)S(1)}, f32[8,128,128]{2,1,0:T(8,128)S(1)}, u32[]{:S(2)}, u32[]{:S(2)}) collective-permute-start(f32[8,128,128]{2,1,0:T(8,128)S(1)} %get-tuple-element.10), channel_id=1, source_target_pairs={{0,8},{8,16},{16,24},{24,32},{32,40},{40,48},{48,56},{56,64},{64,7... | collective-permute-start | bytes 1572872 | tf_op jit(solution)/shard_map/hand_on/ppermute | solution.py:264

commit v2 on v1

v2 whole, which is shorter than its diff:
```python
import jax
import jax.numpy as jnp
from jax import lax
from jax.experimental import pallas as pl
from jax.experimental.pallas import tpu as pltpu
from jax.sharding import Mesh, PartitionSpec as P

ITERS = 4
norm_eps = 1e-06
step_size = 0.5
SITE = ("y2", "y1", "y0", "x1", "x0", "c")
SCAN = ("c", "x0", "x1", "y0", "y1", "y2")
TERM = "z"
VMEM_LIMIT = 24 * 1024 * 1024


def halves(x):
    high = x.astype(jnp.bfloat16)
    low = (x - high.astype(jnp.float32)).astype(jnp.bfloat16)
    return high, low


def mm(a, b):
    return jnp.dot(a, b, preferred_element_type=jnp.float32)


def left_operand(a):
    return jnp.concatenate(halves(a), axis=1)


def right_operand(b):
    high, low = halves(b)
    top = jnp.concatenate([high, low], axis=1)
    return jnp.concatenate([top, top], axis=0)


def joined(a, b):
    both = mm(a, right_operand(b))
    size = b.shape[1]
    return both[:, :size] + both[:, size:]


def total(x):
    return jnp.sum(jnp.sum(x, axis=0, keepdims=True), axis=1, keepdims=True)


def krylov_kernel(z_ref, kept_ref, blocks_ref, prefix_ref, start_ref, basis_ref, moved_ref, sent_ref, left_ref, right_ref):
    groups, per_group, size, _ = blocks_ref.shape
    own = per_group // 2
    terms = groups * own
    prefix = prefix_ref[...]
    forward = left_operand(prefix)
    backward = left_operand(prefix.T)
    square = left_operand(joined(forward, prefix.T))
    squares = jnp.zeros((size, size), jnp.float32)
    for sector in range(start_ref.shape[0]):
        squares = squares + start_ref[sector] * start_ref[sector]
    x = start_ref[z_ref[0]] / jnp.sqrt(total(squares) + norm_eps)
    w = joined(forward, x)
    for group in range(groups):
        for term in range(own):
            at = (group * own + term) * size
            left_ref[at:at + size, :] = left_operand(blocks_ref[group, term])
            high, low = halves(blocks_ref[group, own + term])
            right_ref[at:at + size, :] = jnp.concatenate([high, low], axis=1)
    basis_ref[0] = x
    moved_ref[0] = w
    images = []
    growth = [jnp.ones((1, 1), jnp.float32)]
    for step in range(ITERS):
        middle = joined(left_ref[...], w)
        high, low = halves(middle)
        wide = jnp.concatenate(
            [
                jnp.concatenate([part[t * size:(t + 1) * size] for t in range(terms)], axis=1)
                for part in (high, low)
            ],
            axis=0,
        )
        both = mm(wide, right_ref[...])
        y = (both[:size, :size] + both[size:, size:]) + (both[:size, size:] + both[size:, :size])
        length = jnp.sqrt(total(y * y))
        shrink = jnp.where(length > 0.0, 1.0 / length, 0.0)
        w = joined(square, y) * shrink
        moved_ref[step + 1] = w
        images.append(y * shrink)
        growth.append(growth[step] * length)
    later = joined(backward, jnp.concatenate(images, axis=1))
    basis = [x] + [later[:, step * size:(step + 1) * size] for step in range(ITERS)]
    for step in range(ITERS):
        basis_ref[step + 1] = basis[step + 1]
    blank = jnp.zeros((1, size), jnp.float32)
    across = {}
    for i in range(ITERS + 1):
        for j in range(i, ITERS + 1):
            across[i, j] = across[j, i] = jnp.sum(basis[i] * basis[j], axis=0, keepdims=True)
    across = jnp.concatenate([across.get((i, j), blank) for i in range(8) for j in range(8)], axis=0)
    columns = lax.broadcasted_iota(jnp.int32, (64, size), 1)
    place = lax.broadcasted_iota(jnp.int32, (64, size), 0)
    held = columns < kept_ref[0, z_ref[0]]
    full = jnp.sum(across, axis=1, keepdims=True)
    held = jnp.sum(jnp.where(held, across, 0.0), axis=1, keepdims=True)
    placed = jnp.where(columns == place, full, 0.0) + jnp.where(columns == place + 64, held, 0.0)
    products = jnp.sum(placed, axis=0, keepdims=True)
    lane = lax.broadcasted_iota(jnp.int32, (1, size), 1)
    first, second = jnp.bitwise_and(lane, 56), jnp.bitwise_and(lane, 7)
    grown_first, grown_second = blank, blank
    for j in range(ITERS + 1):
        grown_first = grown_first + jnp.where(first == 8 * j, growth[j], 0.0)
        grown_second = grown_second + jnp.where(second == j, growth[j], 0.0)
    sheet = jnp.concatenate([products, grown_first, grown_second] + [blank] * 5, axis=0)
    for target in range(groups):
        sent_ref[target] = sheet


def combine_kernel(z_ref, kept_ref, scalars_ref, basis_ref, images_ref, moved_ref, sent_ref):
    sectors, _, size = scalars_ref.shape
    tiny = 1e-30

    def over(x):
        return jnp.sum(x, axis=0, keepdims=True)

    def whole(x):
        return jnp.sum(x, axis=1, keepdims=True)

    def earlier(x, count):
        return pltpu.roll(x, size - count, 1)

    def later(x, count):
        return pltpu.roll(x, count, 1)

    grown_first, grown_second = scalars_ref[:, 1, :], scalars_ref[:, 2, :]
    most_first = jnp.maximum(jnp.max(grown_first, axis=0, keepdims=True), tiny)
    most_second = jnp.maximum(jnp.max(grown_second, axis=0, keepdims=True), tiny)
    rate_first = grown_first / most_first
    rate_second = grown_second / most_second
    products = over(scalars_ref[:, 0, :] * rate_first * rate_second)
    lane = lax.broadcasted_iota(jnp.int32, (1, size), 1)
    first, second = jnp.bitwise_and(lane, 56), jnp.bitwise_and(lane, 7)
    ratio_first = jnp.where(first < 8 * ITERS, earlier(most_first, 8) / most_first, 0.0)
    ratio_second = jnp.where(second < ITERS, earlier(most_second, 1) / most_second, 0.0)
    gram = jnp.where(lane < 64, products, 0.0)
    held = jnp.where(lane < 64, 0.0, products)
    on_energy = ratio_second * earlier(gram, 1)
    on_scale = ratio_first * ratio_second * earlier(gram, 9)
    vector_first = jnp.where(first == 0, 1.0, 0.0)
    vector_second = jnp.where(second == 0, 1.0, 0.0)
    square = whole(gram * vector_first * vector_second)
    for step in range(ITERS):
        weights = vector_first * vector_second
        energy = whole(weights * on_energy)
        image_square = whole(weights * on_scale)
        rate = step_size / jnp.sqrt(image_square + norm_eps)
        keep = 1.0 + rate * energy
        update_square = keep * (keep * square - 2.0 * rate * energy) + rate * rate * image_square
        shrink = 1.0 / jnp.sqrt(update_square + norm_eps)
        keep, rate = keep * shrink, rate * shrink
        square = update_square * (shrink * shrink)
        vector_first = keep * vector_first - rate * later(ratio_first * vector_first, 8)
        vector_second = keep * vector_second - rate * later(ratio_second * vector_second, 1)
    masked = whole(held * vector_first * vector_second)
    shrink = 1.0 / jnp.sqrt(jnp.maximum(masked, 0.0) + norm_eps)
    mine = lax.broadcasted_iota(jnp.int32, (sectors, size), 0) == z_ref[0]
    factors = over(jnp.where(mine, rate_first, 0.0)) * vector_first * shrink
    result = jnp.zeros((size, size), jnp.float32)
    moved = jnp.zeros((size, size), jnp.float32)
    for j in range(ITERS + 1):
        factor = factors[:, 8 * j:8 * j + 1]
        result = result + factor * basis_ref[j]
        moved = moved + factor * images_ref[j]
    columns = lax.broadcasted_iota(jnp.int32, (size, size), 1)
    held = columns < kept_ref[0, z_ref[0]]
    result = jnp.where(held, result, 0.0)
    moved = jnp.where(held, moved, 0.0)
    moved_ref[...] = moved
    for target in range(sectors):
        sent_ref[target, 0] = result


def fill_kernel(moved_ref, _, sent_ref):
    for target in range(sent_ref.shape[0]):
        sent_ref[target, 1] = moved_ref[...]


def boundary_kernel(shared_ref, left_ref, psi_ref, out_ref):
    own, sectors, size, _ = left_ref.shape
    for sector in range(sectors):
        psi_ref[0, sector] = shared_ref[sector, 0]
        u = shared_ref[sector, 1]
        right = right_operand(u)
        across = left_operand(u.T)
        for term in range(own):
            half = mm(left_operand(left_ref[term, sector]), right)
            half = half[:, :size] + half[:, size:]
            out_ref[0, term, sector] = joined(across, half)


def vmem():
    return pl.BlockSpec(memory_space=pltpu.VMEM)


def smem():
    return pl.BlockSpec(memory_space=pltpu.SMEM)


def call(kernel, out_shape, in_specs, flops, scratch=(), aliases={}):
    return pl.pallas_call(
        kernel,
        out_shape=out_shape,
        in_specs=in_specs,
        out_specs=jax.tree.map(lambda _: vmem(), out_shape),
        scratch_shapes=scratch,
        input_output_aliases=aliases,
        compiler_params=pltpu.CompilerParams(vmem_limit_bytes=VMEM_LIMIT),
        cost_estimate=pl.CostEstimate(flops=flops, bytes_accessed=4 << 20, transcendentals=0),
    )


def struct(*shape):
    return jax.ShapeDtypeStruct(shape, jnp.float32)


def product(a, b):
    return jnp.dot(a, b, precision=lax.Precision.HIGHEST, preferred_element_type=jnp.float32)


def scanned(own):
    whole = own
    prefix = None
    middle = None
    for level, axis in enumerate(SCAN):
        with jax.named_scope("scan_" + axis):
            pair = lax.all_gather(whole, axis)
            upper = lax.axis_index(axis) == 1
            if prefix is None:
                prefix = jnp.where(upper, pair[0], jnp.eye(own.shape[0], dtype=own.dtype))
            else:
                prefix = jnp.where(upper, product(pair[0], prefix), prefix)
            if level + 1 < len(SCAN):
                whole = product(pair[0], pair[1])
            if axis == "x1":
                middle = whole
    return prefix, middle


def per_device(left_env, right_env, transfer, psi_start, kept):
    left, right, transfer, psi = left_env[0], right_env[0], transfer[0], psi_start[0]
    own, sectors, size, _ = left.shape
    z = lax.axis_index(TERM)
    spot = z[None]
    pairs = [(source, source + 1) for source in range(63)]
    with jax.named_scope("gather_terms"):
        outgoing = jnp.concatenate([left, right], axis=0)
        blocks = lax.all_to_all(outgoing, TERM, 1, 0, tiled=False)
    with jax.named_scope("prefix"):
        prefix, middle = scanned(lax.dynamic_index_in_dim(transfer, z, 0, keepdims=False))
    with jax.named_scope("left_previous"):
        late, _ = lax.optimization_barrier((left, middle))
        left_previous = lax.ppermute(late, SITE, pairs)
    with jax.named_scope("krylov"):
        terms = own * sectors
        prefix, left_previous = lax.optimization_barrier((prefix, left_previous))
        basis, images, sent = call(
            krylov_kernel,
            (struct(ITERS + 1, size, size), struct(ITERS + 1, size, size), struct(sectors, 8, size)),
            [smem(), smem(), vmem(), vmem(), vmem()],
            ITERS * terms * 4 * 2 * 3 * size**3,
            [pltpu.VMEM((terms * size, 2 * size), jnp.bfloat16)] * 2,
        )(spot, kept, blocks, prefix, psi)
    with jax.named_scope("share_scalars"):
        scalars = lax.all_to_all(sent, TERM, 0, 0, tiled=True)
    with jax.named_scope("combine"):
        moved, sent = call(
            combine_kernel,
            (struct(size, size), struct(sectors, 2, size, size)),
            [smem(), smem()] + [vmem()] * 3,
            size**2 * 100,
        )(spot, kept, scalars, basis, images)
    with jax.named_scope("hand_on"):
        moved = lax.ppermute(moved, SITE, pairs)
    with jax.named_scope("share"):
        sent = call(
            fill_kernel,
            struct(sectors, 2, size, size),
            [vmem(), vmem()],
            size**2,
            aliases={1: 0},
        )(moved, sent)
        shared = lax.all_to_all(sent, TERM, 0, 0, tiled=True)
    with jax.named_scope("boundary"):
        result, incoming = call(
            boundary_kernel,
            (struct(1, sectors, size, size), struct(1, own, sectors, size, size)),
            [vmem(), vmem()],
            own * sectors * 12 * size**3,
        )(shared, left_previous)
    return result, incoming


def solution(mesh):
    fine = Mesh(mesh.devices.reshape((2,) * 6 + (8,)), SITE + (TERM,))
    placed = (
        P(SITE, TERM, None, None, None),
        P(SITE, TERM, None, None, None),
        P(SITE, None, None, None),
        P(SITE, None, None, None),
        P(SITE, None),
    )
    return jax.shard_map(
        per_device,
        mesh=fine,
        in_specs=placed,
        out_specs=(P(SITE, None, None, None), P(SITE, TERM, None, None, None)),
        check_vma=False,
    )
```

time: 128 us -> 124 us (0.969)
  the two profiles are of different devices: /device:TPU:32 before, /device:TPU:31 now
where the time goes in v2:
time: 124 us
  blocking collectives  85 us (69%)
  starting transfers between devices  20.6 us (17%)
  Pallas kernels  9.77 us (8%)
  matrix products  2.66 us (2%)
  other arithmetic  1.81 us (1%)
  local copies, waits for them, and re-layouts  1.62 us (1%)
  waiting for transfers between devices  1.32 us (1%)
    all_gather x6, blocking collectives, scanned(): pair = lax.all_gather(whole, axis)  39.8 us
    all_to_all x1, blocking collectives, per_device(): shared = lax.all_to_all(sent, TERM, 0, 0, tiled=True)  31.7 us
    all_to_all x1, blocking collectives, per_device(): scalars = lax.all_to_all(sent, TERM, 0, 0, tiled=True)  13.6 us
    all_to_all x1, starting transfers between devices, per_device(): blocks = lax.all_to_all(outgoing, TERM, 1, 0, tiled=False)  10 us
    ppermute x1, starting transfers between devices, per_device(): left_previous = lax.ppermute(late, SITE, pairs)  6.27 us
    pallas_call x1, Pallas kernels, per_device(): call(krylov_kernel, (struct(ITERS + 1, size, size), struct(ITERS + 1, siz...  5.17 us
    ppermute x1, starting transfers between devices, per_device(): moved = lax.ppermute(moved, SITE, pairs)  4.25 us
    pallas_call x1, Pallas kernels, per_device(): call(boundary_kernel, (struct(1, sectors, size, size), struct(1, own, sec...  3.19 us
  transfers between devices with their start and end apart: 3, of which 1 were waited for; matrix products, arithmetic and copies ran while one was open for 2% of the time, Pallas kernels for 0%

profile of v2, /device:TPU:31, one launch (start us, length us, event | category | flops | bytes accessed | tf_op | source)
XLA Modules:
  0.0 123.6 jit_solution(1116703100532699533)
XLA Ops:
  0.6 0.0 copy-start
  0.6 1.8 %maximum_bitcast_fusion = f32[1,4,8,128,128]{4,3,2,1,0:T(8,128)S(1)} fusion(f32[2,8,128,128]{3,2,1,0:T(8,128)} %bitcast.34, f32[2,8,128,128]{3,2,1,0:T(8,128)} %bitcast.35), kind=kLoop, calls=%fused_computation | loop fusion | flops 524288 | bytes 4194304 | tf_op jit(solution)/shard_map/gather_terms/broadcast_in_dim | solution.py:254
  2.5 1.6 %copy.9 = f32[1,4,8,128,128]{4,3,1,0,2:T(8,128)} copy(f32[1,4,8,128,128]{4,3,2,1,0:T(8,128)S(1)} %maximum_bitcast_fusion) | data formatting | bytes 4194304 | tf_op jit(solution)/shard_map/gather_terms/broadcast_in_dim | solution.py:254
  4.0 10.0 %all-to-all-start = ((f32[1,4,8,128,128]{4,3,1,0,2:T(8,128)}), f32[1,4,8,128,128]{4,3,1,0,2:T(8,128)S(1)}, u32[]{:S(2)}, u32[]{:S(2)}) async-start(f32[1,4,8,128,128]{4,3,1,0,2:T(8,128)} %copy.9), calls=%async_computation | async-start | bytes 4194304 | tf_op jit(solution)/shard_map/gather_terms/all_to_all | solution.py:254
  14.1 0.0 copy-start.1
  14.1 0.0 copy-start.2
  14.1 0.0 copy-done
  14.1 2.6 %all-gather = f32[2,1,128,128]{3,2,1,0:T(8,128)S(1)} all-gather(f32[1,1,128,128]{3,2,1,0:T(8,128)S(1)} %constant_dynamic-slice_fusion), channel_id=2, replica_groups=mesh['y2'=2,'y1'=2,'y0'=2,'x1'=2,'x0'=2,'c'=2,'z'=8] {'c'}, dimensions={0}, use_global_device_ids=true | all-gather | bytes 196608 | tf_op jit(solution)/shard_map/prefix/scan_c/all_gather | solution.py:233
  16.8 0.2 fusion.9
  17.0 4.1 %all-gather.1 = f32[256,128]{1,0:T(8,128)S(1)} all-gather(f32[128,128]{1,0:T(8,128)S(1)} %fusion.9), channel_id=3, replica_groups=mesh['y2'=2,'y1'=2,'y0'=2,'x1'=2,'x0'=2,'c'=2,'z'=8] {'x0'}, dimensions={0}, use_global_device_ids=true | all-gather | bytes 196608 | tf_op jit(solution)/shard_map/prefix/scan_x0/all_gather | solution.py:233
  21.1 0.2 fusion.7
  21.3 5.6 %all-gather.2 = f32[256,128]{1,0:T(8,128)S(1)} all-gather(f32[128,128]{1,0:T(8,128)S(1)} %fusion.7), channel_id=4, replica_groups=mesh['y2'=2,'y1'=2,'y0'=2,'x1'=2,'x0'=2,'c'=2,'z'=8] {'x1'}, dimensions={0}, use_global_device_ids=true | all-gather | bytes 196608 | tf_op jit(solution)/shard_map/prefix/scan_x1/all_gather | solution.py:233
  26.9 0.8 fusion.5
  27.7 6.3 %collective-permute-start = (f32[2,8,128,128]{3,2,1,0:T(8,128)}, f32[2,8,128,128]{3,2,1,0:T(8,128)}, u32[]{:S(2)}, u32[]{:S(2)}) collective-permute-start(f32[2,8,128,128]{3,2,1,0:T(8,128)} %bitcast.36), channel_id=1, source_target_pairs={{0,8},{8,16},{16,24},{24,32},{32,40},{40,48},{48,56},{56,64},{64,7... | collective-permute-start | bytes 3145736 | tf_op jit(solution)/shard_map/left_previous/ppermute | solution.py:259
  34.0 13.7 %all-gather.3 = f32[256,128]{1,0:T(8,128)S(1)} all-gather(f32[128,128]{1,0:T(8,128)} %fusion.5), channel_id=5, replica_groups=mesh['y2'=2,'y1'=2,'y0'=2,'x1'=2,'x0'=2,'c'=2,'z'=8] {'y0'}, dimensions={0}, use_global_device_ids=true | all-gather | bytes 196608 | tf_op jit(solution)/shard_map/prefix/scan_y0/all_gather | solution.py:233
  47.7 0.2 fusion.3
  47.9 5.8 %all-gather.4 = f32[256,128]{1,0:T(8,128)S(1)} all-gather(f32[128,128]{1,0:T(8,128)S(1)} %fusion.3), channel_id=6, replica_groups=mesh['y2'=2,'y1'=2,'y0'=2,'x1'=2,'x0'=2,'c'=2,'z'=8] {'y1'}, dimensions={0}, use_global_device_ids=true | all-gather | bytes 196608 | tf_op jit(solution)/shard_map/prefix/scan_y1/all_gather | solution.py:233
  53.7 0.2 fusion.1
  53.9 8.0 %all-gather.5 = f32[256,128]{1,0:T(8,128)S(1)} all-gather(f32[128,128]{1,0:T(8,128)S(1)} %fusion.1), channel_id=7, replica_groups=mesh['y2'=2,'y1'=2,'y0'=2,'x1'=2,'x0'=2,'c'=2,'z'=8] {'y2'}, dimensions={0}, use_global_device_ids=true | all-gather | bytes 196608 | tf_op jit(solution)/shard_map/prefix/scan_y2/all_gather | solution.py:233
  61.9 0.2 convolution_select_fusion.4
  62.1 0.2 convolution_select_fusion.3
  62.3 0.2 convolution_select_fusion.2
  62.5 0.2 convolution_select_fusion.1
  62.8 0.2 convolution_select_fusion.prefix_ref
  63.0 0.0 collective-permute-done.left_ref
  63.0 0.0 all-to-all-done
  63.0 0.0 copy-done.1
  63.0 0.0 copy-done.2
  63.0 5.2 %krylov.1 = (f32[5,128,128]{2,1,0:T(8,128)S(1)}, f32[5,128,128]{2,1,0:T(8,128)S(1)}, f32[8,8,128]{2,1,0:T(8,128)S(1)}) custom-call(s32[1]{0:T(128)} %bitcast.z_ref, s32[1,8]{1,0:T(1,128)S(1)} %copy-done.1, f32[8,4,128,128]{3,2,1,0:T(8,128)S(1)} %bitcast.32, f32[128,128]{1,0:T(8,128)S(1)} %convolution_select_fusion.prefix_ref, f32[8,128,128]{2,1,0:T(8,128)S(1)} %bitcast.33), custom_call_target="tpu_custom_call" | custom-call | flops 3221225472 | bytes 4194304 | tf_op jit(solution)/shard_map/krylov/pallas_call | solution.py:263
  68.2 13.6 %all_to_all.25.scalars_ref = f32[8,8,128]{2,1,0:T(8,128)S(1)} all-to-all(f32[8,8,128]{2,1,0:T(8,128)S(1)} %get-tuple-element.12), channel_id=1, replica_groups=mesh['y2'=2,'y1'=2,'y0'=2,'x1'=2,'x0'=2,'c'=2,'z'=8] {'z'}, dimensions={0} | all-to-all | bytes 65536 | tf_op jit(solution)/shard_map/share_scalars/all_to_all | solution.py:271
  81.8 1.4 %combine.1 = (f32[128,128]{1,0:T(8,128)S(1)}, f32[8,2,128,128]{3,2,1,0:T(8,128)S(1)}) custom-call(s32[1]{0:T(128)} %bitcast.z_ref, s32[1,8]{1,0:T(1,128)S(1)} %copy-done.1, f32[8,8,128]{2,1,0:T(8,128)S(1)} %all_to_all.25.scalars_ref, f32[5,128,128]{2,1,0:T(8,128)S(1)} %get-tuple-element.13.basis_ref, f32[5,128,128]{2,1,0:T(8,128)S(1)} %get-tuple-element.14.images_ref), custom_call_target="tpu_custom_call" | custom-call | flops 1638400 | bytes 4194304 | tf_op jit(solution)/shard_map/combine/pallas_call | solution.py:273
  83.2 4.3 %collective-permute-start.1 = (f32[128,128]{1,0:T(8,128)S(1)}, f32[128,128]{1,0:T(8,128)S(1)}, u32[]{:S(2)}, u32[]{:S(2)}) collective-permute-start(f32[128,128]{1,0:T(8,128)S(1)} %get-tuple-element.15), channel_id=1, source_target_pairs={{0,8},{8,16},{16,24},{24,32},{32,40},{40,48},{48,56},{56,64},{64,7... | collective-permute-start | bytes 196616 | tf_op jit(solution)/shard_map/hand_on/ppermute | solution.py:280
  87.4 1.3 %collective-permute-done.1.moved_ref = f32[128,128]{1,0:T(8,128)S(1)} collective-permute-done((f32[128,128]{1,0:T(8,128)S(1)}, f32[128,128]{1,0:T(8,128)S(1)}, u32[]{:S(2)}, u32[]{:S(2)}) %collective-permute-start.1) | collective-permute-done | bytes 65568 | tf_op jit(solution)/shard_map/hand_on/ppermute | solution.py:280
  88.8 31.7 %all_to_all.26.shared_ref = f32[8,2,128,128]{3,2,1,0:T(8,128)S(1)} all-to-all(f32[8,2,128,128]{3,2,1,0:T(8,128)S(1)} %share.1), channel_id=1, replica_groups=mesh['y2'=2,'y1'=2,'y0'=2,'x1'=2,'x0'=2,'c'=2,'z'=8] {'z'}, dimensions={0} | all-to-all | bytes 2097152 | tf_op jit(solution)/shard_map/share/all_to_all | solution.py:289
  120.4 3.2 %boundary.1 = (f32[1,8,128,128]{3,2,1,0:T(8,128)}, f32[1,2,8,128,128]{4,3,2,1,0:T(8,128)}) custom-call(f32[8,2,128,128]{3,2,1,0:T(8,128)S(1)} %all_to_all.26.shared_ref, f32[2,8,128,128]{3,2,1,0:T(8,128)} %collective-permute-done.left_ref), custom_call_target="tpu_custom_call" | custom-call | flops 402653184 | bytes 4194304 | tf_op jit(solution)/shard_map/boundary/pallas_call | solution.py:291
  (2 shorter events, 0.0 us)
Async XLA Ops:
  0.6 13.5 %copy-start = (f32[1,8,128,128]{3,2,1,0:T(8,128)S(1)}, f32[1,8,128,128]{3,2,1,0:T(8,128)}, u32[]{:S(2)}) copy-start(f32[1,8,128,128]{3,2,1,0:T(8,128)} %param.7) | copy-start | bytes 1572868
  4.0 58.9 %all-to-all-start = ((f32[1,4,8,128,128]{4,3,1,0,2:T(8,128)}), f32[1,4,8,128,128]{4,3,1,0,2:T(8,128)S(1)}, u32[]{:S(2)}, u32[]{:S(2)}) async-start(f32[1,4,8,128,128]{4,3,1,0,2:T(8,128)} %copy.9), calls=%async_computation | async-start | bytes 4194304 | tf_op jit(solution)/shard_map/gather_terms/all_to_all | solution.py:254
  14.1 48.9 %copy-start.1 = (s32[1,8]{1,0:T(1,128)S(1)}, s32[1,8]{1,0:T(1,128)}, u32[]{:S(2)}) copy-start(s32[1,8]{1,0:T(1,128)} %kept_ref.3) | copy-start | bytes 100
  14.1 48.9 %copy-start.2 = (f32[1,8,128,128]{3,2,1,0:T(8,128)S(1)}, f32[1,8,128,128]{3,2,1,0:T(8,128)}, u32[]{:S(2)}) copy-start(f32[1,8,128,128]{3,2,1,0:T(8,128)} %param.8) | copy-start | bytes 1572868
  27.7 35.3 %collective-permute-start = (f32[2,8,128,128]{3,2,1,0:T(8,128)}, f32[2,8,128,128]{3,2,1,0:T(8,128)}, u32[]{:S(2)}, u32[]{:S(2)}) collective-permute-start(f32[2,8,128,128]{3,2,1,0:T(8,128)} %bitcast.36), channel_id=1, source_target_pairs={{0,8},{8,16},{16,24},{24,32},{32,40},{40,48},{48,56},{56,64},{64,7... | collective-permute-start | bytes 3145736 | tf_op jit(solution)/shard_map/left_previous/ppermute | solution.py:259
  83.2 5.6 %collective-permute-start.1 = (f32[128,128]{1,0:T(8,128)S(1)}, f32[128,128]{1,0:T(8,128)S(1)}, u32[]{:S(2)}, u32[]{:S(2)}) collective-permute-start(f32[128,128]{1,0:T(8,128)S(1)} %get-tuple-element.15), channel_id=1, source_target_pairs={{0,8},{8,16},{16,24},{24,32},{32,40},{40,48},{48,56},{56,64},{64,7... | collective-permute-start | bytes 196616 | tf_op jit(solution)/shard_map/hand_on/ppermute | solution.py:280

commit v3 on v2

--- a/solution.py
+++ b/solution.py
@@ -11,6 +11,9 @@
 SITE = ("y2", "y1", "y0", "x1", "x0", "c")
 SCAN = ("c", "x0", "x1", "y0", "y1", "y2")
 TERM = "z"
+FIRST = (0, 4, 2, 6, 1, 5, 3, 7)
+OWNERS = sum(place << (4 * at) for place, at in enumerate(FIRST))
+LAST = (7, 6, 5, 4, 3, 2, 1, 0)
 VMEM_LIMIT = 24 * 1024 * 1024
 
 
@@ -182,17 +185,25 @@
         sent_ref[target, 1] = moved_ref[...]
 
 
-def boundary_kernel(shared_ref, left_ref, psi_ref, out_ref):
+def boundary_kernel(shared_ref, left_ref, psi_ref, out_ref, made_ref, sems):
     own, sectors, size, _ = left_ref.shape
+    copies = []
     for sector in range(sectors):
-        psi_ref[0, sector] = shared_ref[sector, 0]
-        u = shared_ref[sector, 1]
+        at = LAST.index(FIRST[sector])
+        copies.append(pltpu.make_async_copy(shared_ref.at[at, 0], psi_ref.at[0, sector], sems.at[sector]))
+        copies[-1].start()
+    for sector in range(sectors):
+        u = shared_ref[LAST.index(FIRST[sector]), 1]
         right = right_operand(u)
         across = left_operand(u.T)
         for term in range(own):
             half = mm(left_operand(left_ref[term, sector]), right)
             half = half[:, :size] + half[:, size:]
-            out_ref[0, term, sector] = joined(across, half)
+            made_ref[sector, term] = joined(across, half)
+        copies.append(pltpu.make_async_copy(made_ref.at[sector], out_ref.at[0, :, sector], sems.at[sectors + sector]))
+        copies[-1].start()
+    for copy in copies:
+        copy.wait()
 
 
 def vmem():
@@ -203,12 +214,12 @@
     return pl.BlockSpec(memory_space=pltpu.SMEM)
 
 
-def call(kernel, out_shape, in_specs, flops, scratch=(), aliases={}):
+def call(kernel, out_shape, in_specs, flops, scratch=(), aliases={}, out_spec=pl.BlockSpec(memory_space=pltpu.VMEM)):
     return pl.pallas_call(
         kernel,
         out_shape=out_shape,
         in_specs=in_specs,
-        out_specs=jax.tree.map(lambda _: vmem(), out_shape),
+        out_specs=jax.tree.map(lambda _: out_spec, out_shape),
         scratch_shapes=scratch,
         input_output_aliases=aliases,
         compiler_params=pltpu.CompilerParams(vmem_limit_bytes=VMEM_LIMIT),
@@ -227,7 +238,6 @@
 def scanned(own):
     whole = own
     prefix = None
-    middle = None
     for level, axis in enumerate(SCAN):
         with jax.named_scope("scan_" + axis):
             pair = lax.all_gather(whole, axis)
@@ -238,28 +248,26 @@
                 prefix = jnp.where(upper, product(pair[0], prefix), prefix)
             if level + 1 < len(SCAN):
                 whole = product(pair[0], pair[1])
-            if axis == "x1":
-                middle = whole
-    return prefix, middle
+    return prefix
 
 
 def per_device(left_env, right_env, transfer, psi_start, kept):
     left, right, transfer, psi = left_env[0], right_env[0], transfer[0], psi_start[0]
     own, sectors, size, _ = left.shape
     z = lax.axis_index(TERM)
+    z = jnp.bitwise_and(jnp.right_shift(jnp.int32(OWNERS), 4 * z), 7)
     spot = z[None]
     pairs = [(source, source + 1) for source in range(63)]
     with jax.named_scope("gather_terms"):
         outgoing = jnp.concatenate([left, right], axis=0)
-        blocks = lax.all_to_all(outgoing, TERM, 1, 0, tiled=False)
+        blocks = lax.all_to_all(outgoing, TERM, 1, 0, axis_index_groups=[list(FIRST)], tiled=False)
     with jax.named_scope("prefix"):
-        prefix, middle = scanned(lax.dynamic_index_in_dim(transfer, z, 0, keepdims=False))
+        prefix = scanned(lax.dynamic_index_in_dim(transfer, z, 0, keepdims=False))
     with jax.named_scope("left_previous"):
-        late, _ = lax.optimization_barrier((left, middle))
+        late, _ = lax.optimization_barrier((left, prefix))
         left_previous = lax.ppermute(late, SITE, pairs)
     with jax.named_scope("krylov"):
         terms = own * sectors
-        prefix, left_previous = lax.optimization_barrier((prefix, left_previous))
         basis, images, sent = call(
             krylov_kernel,
             (struct(ITERS + 1, size, size), struct(ITERS + 1, size, size), struct(sectors, 8, size)),
@@ -268,7 +276,7 @@
             [pltpu.VMEM((terms * size, 2 * size), jnp.bfloat16)] * 2,
         )(spot, kept, blocks, prefix, psi)
     with jax.named_scope("share_scalars"):
-        scalars = lax.all_to_all(sent, TERM, 0, 0, tiled=True)
+        scalars = lax.all_to_all(sent, TERM, 0, 0, axis_index_groups=[list(FIRST)], tiled=True)
     with jax.named_scope("combine"):
         moved, sent = call(
             combine_kernel,
@@ -277,6 +285,7 @@
             size**2 * 100,
         )(spot, kept, scalars, basis, images)
     with jax.named_scope("hand_on"):
+        moved, left_previous = lax.optimization_barrier((moved, left_previous))
         moved = lax.ppermute(moved, SITE, pairs)
     with jax.named_scope("share"):
         sent = call(
@@ -286,13 +295,15 @@
             size**2,
             aliases={1: 0},
         )(moved, sent)
-        shared = lax.all_to_all(sent, TERM, 0, 0, tiled=True)
+        shared = lax.all_to_all(sent, TERM, 0, 0, axis_index_groups=[list(LAST)], tiled=True)
     with jax.named_scope("boundary"):
         result, incoming = call(
             boundary_kernel,
             (struct(1, sectors, size, size), struct(1, own, sectors, size, size)),
             [vmem(), vmem()],
             own * sectors * 12 * size**3,
+            [pltpu.VMEM((sectors, own, size, size), jnp.float32), pltpu.SemaphoreType.DMA((2 * sectors,))],
+            out_spec=pl.BlockSpec(memory_space=pl.ANY),
         )(shared, left_previous)
     return result, incoming
 

time: 124 us -> 120 us (0.968)
  the two profiles are of different devices: /device:TPU:31 before, /device:TPU:94 now
where the time goes in v3:
time: 120 us; the launch traced here: 119 us
  blocking collectives  78.2 us (65%)
  starting transfers between devices  13.8 us (12%)
  waiting for transfers between devices  11.6 us (10%)
  Pallas kernels  9.48 us (8%)
  matrix products  2.04 us (2%)
  other arithmetic  1.81 us (2%)
  local copies, waits for them, and re-layouts  1.61 us (1%)
    all_gather x6, blocking collectives, scanned(): pair = lax.all_gather(whole, axis)  33.6 us
    all_to_all x1, blocking collectives, per_device(): lax.all_to_all(sent, TERM, 0, 0, axis_index_groups=[list(LAST)], tiled=True)  30.9 us
    all_to_all x1, blocking collectives, per_device(): lax.all_to_all(sent, TERM, 0, 0, axis_index_groups=[list(FIRST)], tiled=T...  13.6 us
    all_to_all x1, starting transfers between devices, per_device(): lax.all_to_all(outgoing, TERM, 1, 0, axis_index_groups=[list(FIRST)], til...  9.97 us
    all_to_all x1, waiting for transfers between devices, per_device(): lax.all_to_all(outgoing, TERM, 1, 0, axis_index_groups=[list(FIRST)], til...  7.91 us
    pallas_call x1, Pallas kernels, per_device(): call(krylov_kernel, (struct(ITERS + 1, size, size), struct(ITERS + 1, siz...  5.18 us
    ppermute x1, waiting for transfers between devices, per_device(): moved = lax.ppermute(moved, SITE, pairs)  3.66 us
    pallas_call x1, Pallas kernels, per_device(): call(boundary_kernel, (struct(1, sectors, size, size), struct(1, own, sec...  2.9 us
  transfers between devices with their start and end apart: 3, of which 2 were waited for; matrix products, arithmetic and copies ran while one was open for 2% of the time, Pallas kernels for 5%

profile of v3, /device:TPU:94, one launch (start us, length us, event | category | flops | bytes accessed | tf_op | source)
XLA Modules:
  0.0 119.3 jit_solution(12530148594112851985)
XLA Ops:
  0.6 0.0 copy-start
  0.6 1.8 %maximum_bitcast_fusion = f32[1,4,8,128,128]{4,3,2,1,0:T(8,128)S(1)} fusion(f32[2,8,128,128]{3,2,1,0:T(8,128)} %bitcast.34, f32[2,8,128,128]{3,2,1,0:T(8,128)} %bitcast.1), kind=kLoop, calls=%fused_computation | loop fusion | flops 524288 | bytes 4194304 | tf_op jit(solution)/shard_map/gather_terms/broadcast_in_dim | solution.py:263
  2.5 1.6 %copy.9 = f32[1,4,8,128,128]{4,3,1,0,2:T(8,128)} copy(f32[1,4,8,128,128]{4,3,2,1,0:T(8,128)S(1)} %maximum_bitcast_fusion) | data formatting | bytes 4194304 | tf_op jit(solution)/shard_map/gather_terms/broadcast_in_dim | solution.py:263
  4.0 10.0 %all-to-all-start = ((f32[1,4,8,128,128]{4,3,1,0,2:T(8,128)}), f32[1,4,8,128,128]{4,3,1,0,2:T(8,128)S(1)}, u32[]{:S(2)}, u32[]{:S(2)}) async-start(f32[1,4,8,128,128]{4,3,1,0,2:T(8,128)} %copy.9), calls=%async_computation | async-start | bytes 4194304 | tf_op jit(solution)/shard_map/gather_terms/all_to_all | solution.py:263
  14.0 0.0 copy-start.1
  14.0 0.0 copy-start.2
  14.0 0.0 copy-done
  14.0 2.0 %all-gather = f32[2,1,128,128]{3,2,1,0:T(8,128)S(1)} all-gather(f32[1,1,128,128]{3,2,1,0:T(8,128)S(1)} %constant_dynamic-slice_fusion), channel_id=2, replica_groups=mesh['y2'=2,'y1'=2,'y0'=2,'x1'=2,'x0'=2,'c'=2,'z'=8] {'c'}, dimensions={0}, use_global_device_ids=true | all-gather | bytes 196608 | tf_op jit(solution)/shard_map/prefix/scan_c/all_gather | solution.py:243
  16.1 0.2 fusion.9
  16.3 4.9 %all-gather.1 = f32[256,128]{1,0:T(8,128)S(1)} all-gather(f32[128,128]{1,0:T(8,128)S(1)} %fusion.9), channel_id=3, replica_groups=mesh['y2'=2,'y1'=2,'y0'=2,'x1'=2,'x0'=2,'c'=2,'z'=8] {'x0'}, dimensions={0}, use_global_device_ids=true | all-gather | bytes 196608 | tf_op jit(solution)/shard_map/prefix/scan_x0/all_gather | solution.py:243
  21.2 0.2 fusion.7
  21.4 6.4 %all-gather.2 = f32[256,128]{1,0:T(8,128)S(1)} all-gather(f32[128,128]{1,0:T(8,128)S(1)} %fusion.7), channel_id=4, replica_groups=mesh['y2'=2,'y1'=2,'y0'=2,'x1'=2,'x0'=2,'c'=2,'z'=8] {'x1'}, dimensions={0}, use_global_device_ids=true | all-gather | bytes 196608 | tf_op jit(solution)/shard_map/prefix/scan_x1/all_gather | solution.py:243
  27.9 0.2 fusion.5
  28.1 4.9 %all-gather.3 = f32[256,128]{1,0:T(8,128)S(1)} all-gather(f32[128,128]{1,0:T(8,128)S(1)} %fusion.5), channel_id=5, replica_groups=mesh['y2'=2,'y1'=2,'y0'=2,'x1'=2,'x0'=2,'c'=2,'z'=8] {'y0'}, dimensions={0}, use_global_device_ids=true | all-gather | bytes 196608 | tf_op jit(solution)/shard_map/prefix/scan_y0/all_gather | solution.py:243
  33.0 0.2 fusion.3
  33.2 6.4 %all-gather.4 = f32[256,128]{1,0:T(8,128)S(1)} all-gather(f32[128,128]{1,0:T(8,128)S(1)} %fusion.3), channel_id=6, replica_groups=mesh['y2'=2,'y1'=2,'y0'=2,'x1'=2,'x0'=2,'c'=2,'z'=8] {'y1'}, dimensions={0}, use_global_device_ids=true | all-gather | bytes 196608 | tf_op jit(solution)/shard_map/prefix/scan_y1/all_gather | solution.py:243
  39.7 0.2 fusion.1
  39.9 8.8 %all-gather.5 = f32[256,128]{1,0:T(8,128)S(1)} all-gather(f32[128,128]{1,0:T(8,128)S(1)} %fusion.1), channel_id=7, replica_groups=mesh['y2'=2,'y1'=2,'y0'=2,'x1'=2,'x0'=2,'c'=2,'z'=8] {'y2'}, dimensions={0}, use_global_device_ids=true | all-gather | bytes 196608 | tf_op jit(solution)/shard_map/prefix/scan_y2/all_gather | solution.py:243
  48.7 0.2 convolution_select_fusion.4
  48.9 0.2 convolution_select_fusion.3
  49.2 0.2 convolution_select_fusion.2
  49.4 0.2 convolution_select_fusion.1
  49.6 0.2 convolution_select_fusion.prefix_ref
  49.8 1.9 %collective-permute-start = (f32[2,8,128,128]{3,2,1,0:T(8,128)}, f32[2,8,128,128]{3,2,1,0:T(8,128)}, u32[]{:S(2)}, u32[]{:S(2)}) collective-permute-start(f32[2,8,128,128]{3,2,1,0:T(8,128)} %bitcast.1), channel_id=1, source_target_pairs={{0,8},{8,16},{16,24},{24,32},{32,40},{40,48},{48,56},{56,64},{64,7... | collective-permute-start | bytes 3145736 | tf_op jit(solution)/shard_map/left_previous/ppermute | solution.py:268
  51.7 7.9 %all-to-all-done = f32[1,4,8,128,128]{4,3,1,0,2:T(8,128)S(1)} async-done(((f32[1,4,8,128,128]{4,3,1,0,2:T(8,128)}), f32[1,4,8,128,128]{4,3,1,0,2:T(8,128)S(1)}, u32[]{:S(2)}, u32[]{:S(2)}) %all-to-all-start) | async-done | bytes 2097184 | tf_op jit(solution)/shard_map/gather_terms/all_to_all | solution.py:263
  59.7 0.0 copy-done.1
  59.7 0.0 copy-done.2
  59.7 5.2 %krylov.1 = (f32[5,128,128]{2,1,0:T(8,128)S(1)}, f32[5,128,128]{2,1,0:T(8,128)S(1)}, f32[8,8,128]{2,1,0:T(8,128)S(1)}) custom-call(s32[1]{0:T(128)} %bitcast.z_ref, s32[1,8]{1,0:T(1,128)S(1)} %copy-done.1, f32[8,4,128,128]{3,2,1,0:T(8,128)S(1)} %bitcast.32, f32[128,128]{1,0:T(8,128)S(1)} %convolution_select_fusion.prefix_ref, f32[8,128,128]{2,1,0:T(8,128)S(1)} %bitcast.33), custom_call_target="tpu_custom_call" | custom-call | flops 3221225472 | bytes 4194304 | tf_op jit(solution)/shard_map/krylov/pallas_call | solution.py:271
  64.8 13.6 %all_to_all.25.scalars_ref = f32[8,8,128]{2,1,0:T(8,128)S(1)} all-to-all(f32[8,8,128]{2,1,0:T(8,128)S(1)} %get-tuple-element.10), channel_id=1, replica_groups={{0,4,2,6,1,5,3,7},{8,12,10,14,9,13,11,15},{16,20,18,22,17,21,19,23},{24..., dimensions={0} | all-to-all | bytes 65536 | tf_op jit(solution)/shard_map/share_scalars/all_to_all | solution.py:279
  78.5 1.4 %combine.1 = (f32[128,128]{1,0:T(8,128)S(1)}, f32[8,2,128,128]{3,2,1,0:T(8,128)S(1)}) custom-call(s32[1]{0:T(128)} %bitcast.z_ref, s32[1,8]{1,0:T(1,128)S(1)} %copy-done.1, f32[8,8,128]{2,1,0:T(8,128)S(1)} %all_to_all.25.scalars_ref, f32[5,128,128]{2,1,0:T(8,128)S(1)} %get-tuple-element.11.basis_ref, f32[5,128,128]{2,1,0:T(8,128)S(1)} %get-tuple-element.12.images_ref), custom_call_target="tpu_custom_call" | custom-call | flops 1638400 | bytes 4194304 | tf_op jit(solution)/shard_map/combine/pallas_call | solution.py:281
  79.9 0.0 collective-permute-done.left_ref
  79.9 1.9 %collective-permute-start.1 = (f32[128,128]{1,0:T(8,128)S(1)}, f32[128,128]{1,0:T(8,128)S(1)}, u32[]{:S(2)}, u32[]{:S(2)}) collective-permute-start(f32[128,128]{1,0:T(8,128)S(1)} %get-tuple-element.15), channel_id=1, source_target_pairs={{0,8},{8,16},{16,24},{24,32},{32,40},{40,48},{48,56},{56,64},{64,7... | collective-permute-start | bytes 196616 | tf_op jit(solution)/shard_map/hand_on/ppermute | solution.py:289
  81.8 3.7 %collective-permute-done.1.moved_ref = f32[128,128]{1,0:T(8,128)S(1)} collective-permute-done((f32[128,128]{1,0:T(8,128)S(1)}, f32[128,128]{1,0:T(8,128)S(1)}, u32[]{:S(2)}, u32[]{:S(2)}) %collective-permute-start.1) | collective-permute-done | bytes 65568 | tf_op jit(solution)/shard_map/hand_on/ppermute | solution.py:289
  85.5 30.9 %all_to_all.26.shared_ref = f32[8,2,128,128]{3,2,1,0:T(8,128)S(1)} all-to-all(f32[8,2,128,128]{3,2,1,0:T(8,128)S(1)} %share.1), channel_id=1, replica_groups={{7,6,5,4,3,2,1,0},{15,14,13,12,11,10,9,8},{23,22,21,20,19,18,17,16},{31..., dimensions={0} | all-to-all | bytes 2097152 | tf_op jit(solution)/shard_map/share/all_to_all | solution.py:298
  116.4 2.9 %boundary.1 = (f32[1,8,128,128]{3,2,1,0:T(8,128)}, f32[1,2,8,128,128]{4,3,2,1,0:T(8,128)}) custom-call(f32[8,2,128,128]{3,2,1,0:T(8,128)S(1)} %all_to_all.26.shared_ref, f32[2,8,128,128]{3,2,1,0:T(8,128)} %collective-permute-done.left_ref), custom_call_target="tpu_custom_call" | custom-call | flops 402653184 | bytes 4194304 | tf_op jit(solution)/shard_map/boundary/pallas_call | solution.py:300
  (2 shorter events, 0.0 us)
Async XLA Ops:
  0.6 13.4 %copy-start = (f32[1,8,128,128]{3,2,1,0:T(8,128)S(1)}, f32[1,8,128,128]{3,2,1,0:T(8,128)}, u32[]{:S(2)}) copy-start(f32[1,8,128,128]{3,2,1,0:T(8,128)} %param.7) | copy-start | bytes 1572868
  4.0 55.6 %all-to-all-start = ((f32[1,4,8,128,128]{4,3,1,0,2:T(8,128)}), f32[1,4,8,128,128]{4,3,1,0,2:T(8,128)S(1)}, u32[]{:S(2)}, u32[]{:S(2)}) async-start(f32[1,4,8,128,128]{4,3,1,0,2:T(8,128)} %copy.9), calls=%async_computation | async-start | bytes 4194304 | tf_op jit(solution)/shard_map/gather_terms/all_to_all | solution.py:263
  14.0 45.6 %copy-start.1 = (s32[1,8]{1,0:T(1,128)S(1)}, s32[1,8]{1,0:T(1,128)}, u32[]{:S(2)}) copy-start(s32[1,8]{1,0:T(1,128)} %kept_ref.3) | copy-start | bytes 100
  14.0 45.6 %copy-start.2 = (f32[1,8,128,128]{3,2,1,0:T(8,128)S(1)}, f32[1,8,128,128]{3,2,1,0:T(8,128)}, u32[]{:S(2)}) copy-start(f32[1,8,128,128]{3,2,1,0:T(8,128)} %param.8) | copy-start | bytes 1572868
  49.8 30.1 %collective-permute-start = (f32[2,8,128,128]{3,2,1,0:T(8,128)}, f32[2,8,128,128]{3,2,1,0:T(8,128)}, u32[]{:S(2)}, u32[]{:S(2)}) collective-permute-start(f32[2,8,128,128]{3,2,1,0:T(8,128)} %bitcast.1), channel_id=1, source_target_pairs={{0,8},{8,16},{16,24},{24,32},{32,40},{40,48},{48,56},{56,64},{64,7... | collective-permute-start | bytes 3145736 | tf_op jit(solution)/shard_map/left_previous/ppermute | solution.py:268
  79.9 5.6 %collective-permute-start.1 = (f32[128,128]{1,0:T(8,128)S(1)}, f32[128,128]{1,0:T(8,128)S(1)}, u32[]{:S(2)}, u32[]{:S(2)}) collective-permute-start(f32[128,128]{1,0:T(8,128)S(1)} %get-tuple-element.15), channel_id=1, source_target_pairs={{0,8},{8,16},{16,24},{24,32},{32,40},{40,48},{48,56},{56,64},{64,7... | collective-permute-start | bytes 196616 | tf_op jit(solution)/shard_map/hand_on/ppermute | solution.py:289

commit v4 on v3

--- a/solution.py
+++ b/solution.py
@@ -185,6 +185,13 @@
         sent_ref[target, 1] = moved_ref[...]
 
 
+def stage_kernel(left_ref, out_ref):
+    own, sectors, _, _ = left_ref.shape
+    for term in range(own):
+        for sector in range(sectors):
+            out_ref[term, sector] = left_operand(left_ref[term, sector])
+
+
 def boundary_kernel(shared_ref, left_ref, psi_ref, out_ref, made_ref, sems):
     own, sectors, size, _ = left_ref.shape
     copies = []
@@ -197,7 +204,7 @@
         right = right_operand(u)
         across = left_operand(u.T)
         for term in range(own):
-            half = mm(left_operand(left_ref[term, sector]), right)
+            half = mm(left_ref[term, sector], right)
             half = half[:, :size] + half[:, size:]
             made_ref[sector, term] = joined(across, half)
         copies.append(pltpu.make_async_copy(made_ref.at[sector], out_ref.at[0, :, sector], sems.at[sectors + sector]))
@@ -287,6 +294,13 @@
     with jax.named_scope("hand_on"):
         moved, left_previous = lax.optimization_barrier((moved, left_previous))
         moved = lax.ppermute(moved, SITE, pairs)
+        staged = call(
+            stage_kernel,
+            jax.ShapeDtypeStruct((own, sectors, size, 2 * size), jnp.bfloat16),
+            [vmem()],
+            own * sectors * size**3,
+        )(left_previous)
+        moved, staged = lax.optimization_barrier((moved, staged))
     with jax.named_scope("share"):
         sent = call(
             fill_kernel,
@@ -304,7 +318,7 @@
             own * sectors * 12 * size**3,
             [pltpu.VMEM((sectors, own, size, size), jnp.float32), pltpu.SemaphoreType.DMA((2 * sectors,))],
             out_spec=pl.BlockSpec(memory_space=pl.ANY),
-        )(shared, left_previous)
+        )(shared, staged)
     return result, incoming
 
 

time: 120 us -> 119 us (level)
  waiting for transfers between devices: 11.6 us -> 10.2 us
    ppermute x1, waiting for transfers between devices: 3.66 us -> 2.3 us  [per_device(): moved = lax.ppermute(moved, SITE, pairs)]
    pallas_call x0 -> x1, Pallas kernels: none -> 1.35 us  [per_device(): call(stage_kernel, jax.ShapeDtypeStruct((own, sectors, size, 2 * size), j...]
    pallas_call x1, Pallas kernels: 2.9 us -> 1.67 us  [per_device(): call(boundary_kernel, (struct(1, sectors, size, size), struct(1, own, sec...]
  transfers between devices with their start and end apart: 3 -> 3, of which waited for: 2 -> 2; matrix products, arithmetic and copies ran while one was open for 2% -> 2% of each run, Pallas kernels for 5% -> 7%
where the time goes in v4:
time: 119 us; the launch traced here: 118 us
  blocking collectives  78.3 us (66%)
  starting transfers between devices  13.8 us (12%)
  waiting for transfers between devices  10.2 us (9%)
  Pallas kernels  9.61 us (8%)
  matrix products  2.04 us (2%)
  other arithmetic  1.81 us (2%)
  local copies, waits for them, and re-layouts  1.61 us (1%)
    all_gather x6, blocking collectives, scanned(): pair = lax.all_gather(whole, axis)  33.6 us
    all_to_all x1, blocking collectives, per_device(): lax.all_to_all(sent, TERM, 0, 0, axis_index_groups=[list(LAST)], tiled=True)  31 us
    all_to_all x1, blocking collectives, per_device(): lax.all_to_all(sent, TERM, 0, 0, axis_index_groups=[list(FIRST)], tiled=T...  13.6 us
    all_to_all x1, starting transfers between devices, per_device(): lax.all_to_all(outgoing, TERM, 1, 0, axis_index_groups=[list(FIRST)], til...  9.97 us
    all_to_all x1, waiting for transfers between devices, per_device(): lax.all_to_all(outgoing, TERM, 1, 0, axis_index_groups=[list(FIRST)], til...  7.91 us
    pallas_call x1, Pallas kernels, per_device(): call(krylov_kernel, (struct(ITERS + 1, size, size), struct(ITERS + 1, siz...  5.18 us
  transfers between devices with their start and end apart: 3, of which 2 were waited for; matrix products, arithmetic and copies ran while one was open for 2% of the time, Pallas kernels for 7%

profile of v4, /device:TPU:94, one launch (start us, length us, event | category | flops | bytes accessed | tf_op | source)
XLA Modules:
  0.0 118.2 jit_solution(7746262269180187896)
XLA Ops:
  0.6 0.0 copy-start
  0.6 1.8 %maximum_bitcast_fusion = f32[1,4,8,128,128]{4,3,2,1,0:T(8,128)S(1)} fusion(f32[2,8,128,128]{3,2,1,0:T(8,128)} %bitcast.34, f32[2,8,128,128]{3,2,1,0:T(8,128)} %bitcast.1), kind=kLoop, calls=%fused_computation | loop fusion | flops 524288 | bytes 4194304 | tf_op jit(solution)/shard_map/gather_terms/broadcast_in_dim | solution.py:270
  2.5 1.6 %copy.9 = f32[1,4,8,128,128]{4,3,1,0,2:T(8,128)} copy(f32[1,4,8,128,128]{4,3,2,1,0:T(8,128)S(1)} %maximum_bitcast_fusion) | data formatting | bytes 4194304 | tf_op jit(solution)/shard_map/gather_terms/broadcast_in_dim | solution.py:270
  4.0 10.0 %all-to-all-start = ((f32[1,4,8,128,128]{4,3,1,0,2:T(8,128)}), f32[1,4,8,128,128]{4,3,1,0,2:T(8,128)S(1)}, u32[]{:S(2)}, u32[]{:S(2)}) async-start(f32[1,4,8,128,128]{4,3,1,0,2:T(8,128)} %copy.9), calls=%async_computation | async-start | bytes 4194304 | tf_op jit(solution)/shard_map/gather_terms/all_to_all | solution.py:270
  14.0 0.0 copy-start.1
  14.0 0.0 copy-start.2
  14.0 0.0 copy-done
  14.0 2.0 %all-gather = f32[2,1,128,128]{3,2,1,0:T(8,128)S(1)} all-gather(f32[1,1,128,128]{3,2,1,0:T(8,128)S(1)} %constant_dynamic-slice_fusion), channel_id=2, replica_groups=mesh['y2'=2,'y1'=2,'y0'=2,'x1'=2,'x0'=2,'c'=2,'z'=8] {'c'}, dimensions={0}, use_global_device_ids=true | all-gather | bytes 196608 | tf_op jit(solution)/shard_map/prefix/scan_c/all_gather | solution.py:250
  16.1 0.2 fusion.9
  16.3 4.9 %all-gather.1 = f32[256,128]{1,0:T(8,128)S(1)} all-gather(f32[128,128]{1,0:T(8,128)S(1)} %fusion.9), channel_id=3, replica_groups=mesh['y2'=2,'y1'=2,'y0'=2,'x1'=2,'x0'=2,'c'=2,'z'=8] {'x0'}, dimensions={0}, use_global_device_ids=true | all-gather | bytes 196608 | tf_op jit(solution)/shard_map/prefix/scan_x0/all_gather | solution.py:250
  21.2 0.2 fusion.7
  21.4 6.4 %all-gather.2 = f32[256,128]{1,0:T(8,128)S(1)} all-gather(f32[128,128]{1,0:T(8,128)S(1)} %fusion.7), channel_id=4, replica_groups=mesh['y2'=2,'y1'=2,'y0'=2,'x1'=2,'x0'=2,'c'=2,'z'=8] {'x1'}, dimensions={0}, use_global_device_ids=true | all-gather | bytes 196608 | tf_op jit(solution)/shard_map/prefix/scan_x1/all_gather | solution.py:250
  27.9 0.2 fusion.5
  28.1 4.9 %all-gather.3 = f32[256,128]{1,0:T(8,128)S(1)} all-gather(f32[128,128]{1,0:T(8,128)S(1)} %fusion.5), channel_id=5, replica_groups=mesh['y2'=2,'y1'=2,'y0'=2,'x1'=2,'x0'=2,'c'=2,'z'=8] {'y0'}, dimensions={0}, use_global_device_ids=true | all-gather | bytes 196608 | tf_op jit(solution)/shard_map/prefix/scan_y0/all_gather | solution.py:250
  33.0 0.2 fusion.3
  33.2 6.4 %all-gather.4 = f32[256,128]{1,0:T(8,128)S(1)} all-gather(f32[128,128]{1,0:T(8,128)S(1)} %fusion.3), channel_id=6, replica_groups=mesh['y2'=2,'y1'=2,'y0'=2,'x1'=2,'x0'=2,'c'=2,'z'=8] {'y1'}, dimensions={0}, use_global_device_ids=true | all-gather | bytes 196608 | tf_op jit(solution)/shard_map/prefix/scan_y1/all_gather | solution.py:250
  39.7 0.2 fusion.1
  39.9 8.8 %all-gather.5 = f32[256,128]{1,0:T(8,128)S(1)} all-gather(f32[128,128]{1,0:T(8,128)S(1)} %fusion.1), channel_id=7, replica_groups=mesh['y2'=2,'y1'=2,'y0'=2,'x1'=2,'x0'=2,'c'=2,'z'=8] {'y2'}, dimensions={0}, use_global_device_ids=true | all-gather | bytes 196608 | tf_op jit(solution)/shard_map/prefix/scan_y2/all_gather | solution.py:250
  48.7 0.2 convolution_select_fusion.4
  48.9 0.2 convolution_select_fusion.3
  49.2 0.2 convolution_select_fusion.2
  49.4 0.2 convolution_select_fusion.1
  49.6 0.2 convolution_select_fusion.prefix_ref
  49.8 1.9 %collective-permute-start = (f32[2,8,128,128]{3,2,1,0:T(8,128)}, f32[2,8,128,128]{3,2,1,0:T(8,128)}, u32[]{:S(2)}, u32[]{:S(2)}) collective-permute-start(f32[2,8,128,128]{3,2,1,0:T(8,128)} %bitcast.1), channel_id=1, source_target_pairs={{0,8},{8,16},{16,24},{24,32},{32,40},{40,48},{48,56},{56,64},{64,7... | collective-permute-start | bytes 3145736 | tf_op jit(solution)/shard_map/left_previous/ppermute | solution.py:275
  51.7 7.9 %all-to-all-done = f32[1,4,8,128,128]{4,3,1,0,2:T(8,128)S(1)} async-done(((f32[1,4,8,128,128]{4,3,1,0,2:T(8,128)}), f32[1,4,8,128,128]{4,3,1,0,2:T(8,128)S(1)}, u32[]{:S(2)}, u32[]{:S(2)}) %all-to-all-start) | async-done | bytes 2097184 | tf_op jit(solution)/shard_map/gather_terms/all_to_all | solution.py:270
  59.7 0.0 copy-done.1
  59.7 0.0 copy-done.2
  59.7 5.2 %krylov.1 = (f32[5,128,128]{2,1,0:T(8,128)S(1)}, f32[5,128,128]{2,1,0:T(8,128)S(1)}, f32[8,8,128]{2,1,0:T(8,128)S(1)}) custom-call(s32[1]{0:T(128)} %bitcast.z_ref, s32[1,8]{1,0:T(1,128)S(1)} %copy-done.1, f32[8,4,128,128]{3,2,1,0:T(8,128)S(1)} %bitcast.32, f32[128,128]{1,0:T(8,128)S(1)} %convolution_select_fusion.prefix_ref, f32[8,128,128]{2,1,0:T(8,128)S(1)} %bitcast.33), custom_call_target="tpu_custom_call" | custom-call | flops 3221225472 | bytes 4194304 | tf_op jit(solution)/shard_map/krylov/pallas_call | solution.py:278
  64.8 13.6 %all_to_all.25.scalars_ref = f32[8,8,128]{2,1,0:T(8,128)S(1)} all-to-all(f32[8,8,128]{2,1,0:T(8,128)S(1)} %get-tuple-element.12), channel_id=1, replica_groups={{0,4,2,6,1,5,3,7},{8,12,10,14,9,13,11,15},{16,20,18,22,17,21,19,23},{24..., dimensions={0} | all-to-all | bytes 65536 | tf_op jit(solution)/shard_map/share_scalars/all_to_all | solution.py:286
  78.5 1.4 %combine.1 = (f32[128,128]{1,0:T(8,128)S(1)}, f32[8,2,128,128]{3,2,1,0:T(8,128)S(1)}) custom-call(s32[1]{0:T(128)} %bitcast.z_ref, s32[1,8]{1,0:T(1,128)S(1)} %copy-done.1, f32[8,8,128]{2,1,0:T(8,128)S(1)} %all_to_all.25.scalars_ref, f32[5,128,128]{2,1,0:T(8,128)S(1)} %get-tuple-element.13.basis_ref, f32[5,128,128]{2,1,0:T(8,128)S(1)} %get-tuple-element.14.images_ref), custom_call_target="tpu_custom_call" | custom-call | flops 1638400 | bytes 4194304 | tf_op jit(solution)/shard_map/combine/pallas_call | solution.py:288
  79.9 0.0 collective-permute-done.left_ref
  79.9 1.9 %collective-permute-start.1 = (f32[128,128]{1,0:T(8,128)S(1)}, f32[128,128]{1,0:T(8,128)S(1)}, u32[]{:S(2)}, u32[]{:S(2)}) collective-permute-start(f32[128,128]{1,0:T(8,128)S(1)} %get-tuple-element.17), channel_id=1, source_target_pairs={{0,8},{8,16},{16,24},{24,32},{32,40},{40,48},{48,56},{56,64},{64,7... | collective-permute-start | bytes 196616 | tf_op jit(solution)/shard_map/hand_on/ppermute | solution.py:296
  81.8 1.4 %hand_on.1.left_ref = bf16[2,8,128,256]{3,2,1,0:T(8,128)(2,1)S(1)} custom-call(f32[2,8,128,128]{3,2,1,0:T(8,128)} %collective-permute-done.left_ref), custom_call_target="tpu_custom_call" | custom-call | flops 33554432 | bytes 4194304 | tf_op jit(solution)/shard_map/hand_on/pallas_call | solution.py:297
  83.2 2.3 %collective-permute-done.1.moved_ref = f32[128,128]{1,0:T(8,128)S(1)} collective-permute-done((f32[128,128]{1,0:T(8,128)S(1)}, f32[128,128]{1,0:T(8,128)S(1)}, u32[]{:S(2)}, u32[]{:S(2)}) %collective-permute-start.1) | collective-permute-done | bytes 65568 | tf_op jit(solution)/shard_map/hand_on/ppermute | solution.py:296
  85.5 31.0 %all_to_all.26.shared_ref = f32[8,2,128,128]{3,2,1,0:T(8,128)S(1)} all-to-all(f32[8,2,128,128]{3,2,1,0:T(8,128)S(1)} %share.1), channel_id=1, replica_groups={{7,6,5,4,3,2,1,0},{15,14,13,12,11,10,9,8},{23,22,21,20,19,18,17,16},{31..., dimensions={0} | all-to-all | bytes 2097152 | tf_op jit(solution)/shard_map/share/all_to_all | solution.py:312
  116.5 1.7 %boundary.1 = (f32[1,8,128,128]{3,2,1,0:T(8,128)}, f32[1,2,8,128,128]{4,3,2,1,0:T(8,128)}) custom-call(f32[8,2,128,128]{3,2,1,0:T(8,128)S(1)} %all_to_all.26.shared_ref, bf16[2,8,128,256]{3,2,1,0:T(8,128)(2,1)S(1)} %hand_on.1.left_ref), custom_call_target="tpu_custom_call" | custom-call | flops 402653184 | bytes 4194304 | tf_op jit(solution)/shard_map/boundary/pallas_call | solution.py:314
  (2 shorter events, 0.0 us)
Async XLA Ops:
  0.6 13.4 %copy-start = (f32[1,8,128,128]{3,2,1,0:T(8,128)S(1)}, f32[1,8,128,128]{3,2,1,0:T(8,128)}, u32[]{:S(2)}) copy-start(f32[1,8,128,128]{3,2,1,0:T(8,128)} %param.7) | copy-start | bytes 1572868
  4.0 55.6 %all-to-all-start = ((f32[1,4,8,128,128]{4,3,1,0,2:T(8,128)}), f32[1,4,8,128,128]{4,3,1,0,2:T(8,128)S(1)}, u32[]{:S(2)}, u32[]{:S(2)}) async-start(f32[1,4,8,128,128]{4,3,1,0,2:T(8,128)} %copy.9), calls=%async_computation | async-start | bytes 4194304 | tf_op jit(solution)/shard_map/gather_terms/all_to_all | solution.py:270
  14.0 45.6 %copy-start.1 = (s32[1,8]{1,0:T(1,128)S(1)}, s32[1,8]{1,0:T(1,128)}, u32[]{:S(2)}) copy-start(s32[1,8]{1,0:T(1,128)} %kept_ref.3) | copy-start | bytes 100
  14.0 45.6 %copy-start.2 = (f32[1,8,128,128]{3,2,1,0:T(8,128)S(1)}, f32[1,8,128,128]{3,2,1,0:T(8,128)}, u32[]{:S(2)}) copy-start(f32[1,8,128,128]{3,2,1,0:T(8,128)} %param.8) | copy-start | bytes 1572868
  49.8 30.1 %collective-permute-start = (f32[2,8,128,128]{3,2,1,0:T(8,128)}, f32[2,8,128,128]{3,2,1,0:T(8,128)}, u32[]{:S(2)}, u32[]{:S(2)}) collective-permute-start(f32[2,8,128,128]{3,2,1,0:T(8,128)} %bitcast.1), channel_id=1, source_target_pairs={{0,8},{8,16},{16,24},{24,32},{32,40},{40,48},{48,56},{56,64},{64,7... | collective-permute-start | bytes 3145736 | tf_op jit(solution)/shard_map/left_previous/ppermute | solution.py:275
  79.9 5.6 %collective-permute-start.1 = (f32[128,128]{1,0:T(8,128)S(1)}, f32[128,128]{1,0:T(8,128)S(1)}, u32[]{:S(2)}, u32[]{:S(2)}) collective-permute-start(f32[128,128]{1,0:T(8,128)S(1)} %get-tuple-element.17), channel_id=1, source_target_pairs={{0,8},{8,16},{16,24},{24,32},{32,40},{40,48},{48,56},{56,64},{64,7... | collective-permute-start | bytes 196616 | tf_op jit(solution)/shard_map/hand_on/ppermute | solution.py:296

commit v5 on v4

--- a/solution.py
+++ b/solution.py
@@ -11,7 +11,7 @@
 SITE = ("y2", "y1", "y0", "x1", "x0", "c")
 SCAN = ("c", "x0", "x1", "y0", "y1", "y2")
 TERM = "z"
-FIRST = (0, 4, 2, 6, 1, 5, 3, 7)
+FIRST = (0, 4, 1, 5, 2, 6, 3, 7)
 OWNERS = sum(place << (4 * at) for place, at in enumerate(FIRST))
 LAST = (7, 6, 5, 4, 3, 2, 1, 0)
 VMEM_LIMIT = 24 * 1024 * 1024
@@ -47,19 +47,26 @@
     return jnp.sum(jnp.sum(x, axis=0, keepdims=True), axis=1, keepdims=True)
 
 
-def krylov_kernel(z_ref, kept_ref, blocks_ref, prefix_ref, start_ref, basis_ref, moved_ref, sent_ref, left_ref, right_ref):
+def prepare_kernel(z_ref, prefix_ref, start_ref, x_ref, w_ref, backward_ref, square_ref):
+    sectors, size, _ = start_ref.shape
+    prefix = prefix_ref[...]
+    forward = left_operand(prefix)
+    backward_ref[...] = left_operand(prefix.T)
+    square_ref[...] = left_operand(joined(forward, prefix.T))
+    squares = jnp.zeros((size, size), jnp.float32)
+    for sector in range(sectors):
+        squares = squares + start_ref[sector] * start_ref[sector]
+    x = start_ref[z_ref[0]] / jnp.sqrt(total(squares) + norm_eps)
+    x_ref[...] = x
+    w_ref[...] = joined(forward, x)
+
+
+def krylov_kernel(z_ref, kept_ref, blocks_ref, x_ref, w_ref, backward_ref, square_ref, basis_ref, moved_ref, sent_ref, left_ref, right_ref):
     groups, per_group, size, _ = blocks_ref.shape
     own = per_group // 2
     terms = groups * own
-    prefix = prefix_ref[...]
-    forward = left_operand(prefix)
-    backward = left_operand(prefix.T)
-    square = left_operand(joined(forward, prefix.T))
-    squares = jnp.zeros((size, size), jnp.float32)
-    for sector in range(start_ref.shape[0]):
-        squares = squares + start_ref[sector] * start_ref[sector]
-    x = start_ref[z_ref[0]] / jnp.sqrt(total(squares) + norm_eps)
-    w = joined(forward, x)
+    x, w = x_ref[...], w_ref[...]
+    backward, square = backward_ref[...], square_ref[...]
     for group in range(groups):
         for term in range(own):
             at = (group * own + term) * size
@@ -273,15 +280,23 @@
     with jax.named_scope("left_previous"):
         late, _ = lax.optimization_barrier((left, prefix))
         left_previous = lax.ppermute(late, SITE, pairs)
+    with jax.named_scope("prepare"):
+        operand = jax.ShapeDtypeStruct((size, 2 * size), jnp.bfloat16)
+        ready = call(
+            prepare_kernel,
+            (struct(size, size), struct(size, size), operand, operand),
+            [smem(), vmem(), vmem()],
+            20 * size**3,
+        )(spot, prefix, psi)
     with jax.named_scope("krylov"):
         terms = own * sectors
         basis, images, sent = call(
             krylov_kernel,
             (struct(ITERS + 1, size, size), struct(ITERS + 1, size, size), struct(sectors, 8, size)),
-            [smem(), smem(), vmem(), vmem(), vmem()],
+            [smem(), smem()] + [vmem()] * 5,
             ITERS * terms * 4 * 2 * 3 * size**3,
             [pltpu.VMEM((terms * size, 2 * size), jnp.bfloat16)] * 2,
-        )(spot, kept, blocks, prefix, psi)
+        )(spot, kept, blocks, *ready)
     with jax.named_scope("share_scalars"):
         scalars = lax.all_to_all(sent, TERM, 0, 0, axis_index_groups=[list(FIRST)], tiled=True)
     with jax.named_scope("combine"):

time: 119 us -> 118 us (level)
  blocking collectives: 78.3 us -> 74.8 us
  waiting for transfers between devices: 10.2 us -> 13.3 us
    all_to_all x1, blocking collectives: 13.6 us -> 10.3 us  [per_device(): lax.all_to_all(sent, TERM, 0, 0, axis_index_groups=[list(FIRST)], tiled=T...]
    all_to_all x1, waiting for transfers between devices: 7.91 us -> 11 us  [per_device(): lax.all_to_all(outgoing, TERM, 1, 0, axis_index_groups=[list(FIRST)], til...]
where the time goes in v5:
time: 118 us
  blocking collectives  74.8 us (63%)
  starting transfers between devices  13.8 us (12%)
  waiting for transfers between devices  13.3 us (11%)
  Pallas kernels  9.65 us (8%)
  matrix products  2.04 us (2%)
  other arithmetic  1.81 us (2%)
  local copies, waits for them, and re-layouts  1.61 us (1%)
    all_gather x6, blocking collectives, scanned(): pair = lax.all_gather(whole, axis)  33.6 us
    all_to_all x1, blocking collectives, per_device(): lax.all_to_all(sent, TERM, 0, 0, axis_index_groups=[list(LAST)], tiled=True)  30.9 us
    all_to_all x1, waiting for transfers between devices, per_device(): lax.all_to_all(outgoing, TERM, 1, 0, axis_index_groups=[list(FIRST)], til...  11 us
    all_to_all x1, blocking collectives, per_device(): lax.all_to_all(sent, TERM, 0, 0, axis_index_groups=[list(FIRST)], tiled=T...  10.3 us
    all_to_all x1, starting transfers between devices, per_device(): lax.all_to_all(outgoing, TERM, 1, 0, axis_index_groups=[list(FIRST)], til...  9.97 us
    pallas_call x1, Pallas kernels, per_device(): call(krylov_kernel, (struct(ITERS + 1, size, size), struct(ITERS + 1, siz...  4.87 us
  transfers between devices with their start and end apart: 3, of which 2 were waited for; matrix products, arithmetic and copies ran while one was open for 2% of the time, Pallas kernels for 7%

profile of v5, /device:TPU:94, one launch (start us, length us, event | category | flops | bytes accessed | tf_op | source)
XLA Modules:
  0.0 117.8 jit_solution(1732964881114091588)
XLA Ops:
  0.6 0.0 copy-start
  0.6 1.8 %maximum_bitcast_fusion = f32[1,4,8,128,128]{4,3,2,1,0:T(8,128)S(1)} fusion(f32[2,8,128,128]{3,2,1,0:T(8,128)} %bitcast.34, f32[2,8,128,128]{3,2,1,0:T(8,128)} %bitcast.1), kind=kLoop, calls=%fused_computation | loop fusion | flops 524288 | bytes 4194304 | tf_op jit(solution)/shard_map/gather_terms/broadcast_in_dim | solution.py:277
  2.5 1.6 %copy.9 = f32[1,4,8,128,128]{4,3,1,0,2:T(8,128)} copy(f32[1,4,8,128,128]{4,3,2,1,0:T(8,128)S(1)} %maximum_bitcast_fusion) | data formatting | bytes 4194304 | tf_op jit(solution)/shard_map/gather_terms/broadcast_in_dim | solution.py:277
  4.0 10.0 %all-to-all-start = ((f32[1,4,8,128,128]{4,3,1,0,2:T(8,128)}), f32[1,4,8,128,128]{4,3,1,0,2:T(8,128)S(1)}, u32[]{:S(2)}, u32[]{:S(2)}) async-start(f32[1,4,8,128,128]{4,3,1,0,2:T(8,128)} %copy.9), calls=%async_computation | async-start | bytes 4194304 | tf_op jit(solution)/shard_map/gather_terms/all_to_all | solution.py:277
  14.0 0.0 copy-start.1
  14.0 0.0 copy-start.2
  14.0 0.0 copy-done
  14.0 2.0 %all-gather = f32[2,1,128,128]{3,2,1,0:T(8,128)S(1)} all-gather(f32[1,1,128,128]{3,2,1,0:T(8,128)S(1)} %constant_dynamic-slice_fusion), channel_id=2, replica_groups=mesh['y2'=2,'y1'=2,'y0'=2,'x1'=2,'x0'=2,'c'=2,'z'=8] {'c'}, dimensions={0}, use_global_device_ids=true | all-gather | bytes 196608 | tf_op jit(solution)/shard_map/prefix/scan_c/all_gather | solution.py:257
  16.1 0.2 fusion.9
  16.3 4.9 %all-gather.1 = f32[256,128]{1,0:T(8,128)S(1)} all-gather(f32[128,128]{1,0:T(8,128)S(1)} %fusion.9), channel_id=3, replica_groups=mesh['y2'=2,'y1'=2,'y0'=2,'x1'=2,'x0'=2,'c'=2,'z'=8] {'x0'}, dimensions={0}, use_global_device_ids=true | all-gather | bytes 196608 | tf_op jit(solution)/shard_map/prefix/scan_x0/all_gather | solution.py:257
  21.2 0.2 fusion.7
  21.4 6.4 %all-gather.2 = f32[256,128]{1,0:T(8,128)S(1)} all-gather(f32[128,128]{1,0:T(8,128)S(1)} %fusion.7), channel_id=4, replica_groups=mesh['y2'=2,'y1'=2,'y0'=2,'x1'=2,'x0'=2,'c'=2,'z'=8] {'x1'}, dimensions={0}, use_global_device_ids=true | all-gather | bytes 196608 | tf_op jit(solution)/shard_map/prefix/scan_x1/all_gather | solution.py:257
  27.9 0.2 fusion.5
  28.1 4.9 %all-gather.3 = f32[256,128]{1,0:T(8,128)S(1)} all-gather(f32[128,128]{1,0:T(8,128)S(1)} %fusion.5), channel_id=5, replica_groups=mesh['y2'=2,'y1'=2,'y0'=2,'x1'=2,'x0'=2,'c'=2,'z'=8] {'y0'}, dimensions={0}, use_global_device_ids=true | all-gather | bytes 196608 | tf_op jit(solution)/shard_map/prefix/scan_y0/all_gather | solution.py:257
  33.0 0.2 fusion.3
  33.2 6.4 %all-gather.4 = f32[256,128]{1,0:T(8,128)S(1)} all-gather(f32[128,128]{1,0:T(8,128)S(1)} %fusion.3), channel_id=6, replica_groups=mesh['y2'=2,'y1'=2,'y0'=2,'x1'=2,'x0'=2,'c'=2,'z'=8] {'y1'}, dimensions={0}, use_global_device_ids=true | all-gather | bytes 196608 | tf_op jit(solution)/shard_map/prefix/scan_y1/all_gather | solution.py:257
  39.7 0.2 fusion.1
  39.9 8.8 %all-gather.5 = f32[256,128]{1,0:T(8,128)S(1)} all-gather(f32[128,128]{1,0:T(8,128)S(1)} %fusion.1), channel_id=7, replica_groups=mesh['y2'=2,'y1'=2,'y0'=2,'x1'=2,'x0'=2,'c'=2,'z'=8] {'y2'}, dimensions={0}, use_global_device_ids=true | all-gather | bytes 196608 | tf_op jit(solution)/shard_map/prefix/scan_y2/all_gather | solution.py:257
  48.7 0.2 convolution_select_fusion.4
  48.9 0.2 convolution_select_fusion.3
  49.2 0.2 convolution_select_fusion.2
  49.4 0.2 convolution_select_fusion.1
  49.6 0.2 convolution_select_fusion.prefix_ref
  49.8 1.9 %collective-permute-start = (f32[2,8,128,128]{3,2,1,0:T(8,128)}, f32[2,8,128,128]{3,2,1,0:T(8,128)}, u32[]{:S(2)}, u32[]{:S(2)}) collective-permute-start(f32[2,8,128,128]{3,2,1,0:T(8,128)} %bitcast.1), channel_id=1, source_target_pairs={{0,8},{8,16},{16,24},{24,32},{32,40},{40,48},{48,56},{56,64},{64,7... | collective-permute-start | bytes 3145736 | tf_op jit(solution)/shard_map/left_previous/ppermute | solution.py:282
  51.7 0.0 copy-done.1
  51.7 0.3 prepare.1
  52.1 11.0 %all-to-all-done = f32[1,4,8,128,128]{4,3,1,0,2:T(8,128)S(1)} async-done(((f32[1,4,8,128,128]{4,3,1,0,2:T(8,128)}), f32[1,4,8,128,128]{4,3,1,0,2:T(8,128)S(1)}, u32[]{:S(2)}, u32[]{:S(2)}) %all-to-all-start) | async-done | bytes 2097184 | tf_op jit(solution)/shard_map/gather_terms/all_to_all | solution.py:277
  63.1 0.0 copy-done.2
  63.1 4.9 %krylov.1 = (f32[5,128,128]{2,1,0:T(8,128)S(1)}, f32[5,128,128]{2,1,0:T(8,128)S(1)}, f32[8,8,128]{2,1,0:T(8,128)S(1)}) custom-call(s32[1]{0:T(128)} %bitcast.z_ref, s32[1,8]{1,0:T(1,128)S(1)} %copy-done.2, f32[8,4,128,128]{3,2,1,0:T(8,128)S(1)} %bitcast.32, f32[128,128]{1,0:T(8,128)S(1)} %get-tuple-element.16.x_ref, f32[128,128]{1,0:T(8,128)S(1)} %get-tuple-element.17.w_ref, ...), custom_call_target="tpu_custom_call" | custom-call | flops 3221225472 | bytes 4194304 | tf_op jit(solution)/shard_map/krylov/pallas_call | solution.py:293
  68.0 10.3 %all_to_all.25.scalars_ref = f32[8,8,128]{2,1,0:T(8,128)S(1)} all-to-all(f32[8,8,128]{2,1,0:T(8,128)S(1)} %get-tuple-element.20), channel_id=1, replica_groups={{0,4,1,5,2,6,3,7},{8,12,9,13,10,14,11,15},{16,20,17,21,18,22,19,23},{24..., dimensions={0} | all-to-all | bytes 65536 | tf_op jit(solution)/shard_map/share_scalars/all_to_all | solution.py:301
  78.3 1.4 %combine.1 = (f32[128,128]{1,0:T(8,128)S(1)}, f32[8,2,128,128]{3,2,1,0:T(8,128)S(1)}) custom-call(s32[1]{0:T(128)} %bitcast.z_ref, s32[1,8]{1,0:T(1,128)S(1)} %copy-done.2, f32[8,8,128]{2,1,0:T(8,128)S(1)} %all_to_all.25.scalars_ref, f32[5,128,128]{2,1,0:T(8,128)S(1)} %get-tuple-element.21.basis_ref, f32[5,128,128]{2,1,0:T(8,128)S(1)} %get-tuple-element.22.images_ref), custom_call_target="tpu_custom_call" | custom-call | flops 1638400 | bytes 4194304 | tf_op jit(solution)/shard_map/combine/pallas_call | solution.py:303
  79.7 0.0 collective-permute-done.left_ref
  79.7 1.9 %collective-permute-start.1 = (f32[128,128]{1,0:T(8,128)S(1)}, f32[128,128]{1,0:T(8,128)S(1)}, u32[]{:S(2)}, u32[]{:S(2)}) collective-permute-start(f32[128,128]{1,0:T(8,128)S(1)} %get-tuple-element.25), channel_id=1, source_target_pairs={{0,8},{8,16},{16,24},{24,32},{32,40},{40,48},{48,56},{56,64},{64,7... | collective-permute-start | bytes 196616 | tf_op jit(solution)/shard_map/hand_on/ppermute | solution.py:311
  81.6 1.4 %hand_on.1.left_ref = bf16[2,8,128,256]{3,2,1,0:T(8,128)(2,1)S(1)} custom-call(f32[2,8,128,128]{3,2,1,0:T(8,128)} %collective-permute-done.left_ref), custom_call_target="tpu_custom_call" | custom-call | flops 33554432 | bytes 4194304 | tf_op jit(solution)/shard_map/hand_on/pallas_call | solution.py:312
  83.0 2.3 %collective-permute-done.1.moved_ref = f32[128,128]{1,0:T(8,128)S(1)} collective-permute-done((f32[128,128]{1,0:T(8,128)S(1)}, f32[128,128]{1,0:T(8,128)S(1)}, u32[]{:S(2)}, u32[]{:S(2)}) %collective-permute-start.1) | collective-permute-done | bytes 65568 | tf_op jit(solution)/shard_map/hand_on/ppermute | solution.py:311
  85.3 30.9 %all_to_all.26.shared_ref = f32[8,2,128,128]{3,2,1,0:T(8,128)S(1)} all-to-all(f32[8,2,128,128]{3,2,1,0:T(8,128)S(1)} %share.1), channel_id=1, replica_groups={{7,6,5,4,3,2,1,0},{15,14,13,12,11,10,9,8},{23,22,21,20,19,18,17,16},{31..., dimensions={0} | all-to-all | bytes 2097152 | tf_op jit(solution)/shard_map/share/all_to_all | solution.py:327
  116.2 1.7 %boundary.1 = (f32[1,8,128,128]{3,2,1,0:T(8,128)}, f32[1,2,8,128,128]{4,3,2,1,0:T(8,128)}) custom-call(f32[8,2,128,128]{3,2,1,0:T(8,128)S(1)} %all_to_all.26.shared_ref, bf16[2,8,128,256]{3,2,1,0:T(8,128)(2,1)S(1)} %hand_on.1.left_ref), custom_call_target="tpu_custom_call" | custom-call | flops 402653184 | bytes 4194304 | tf_op jit(solution)/shard_map/boundary/pallas_call | solution.py:329
  (2 shorter events, 0.0 us)
Async XLA Ops:
  0.6 13.4 %copy-start = (f32[1,8,128,128]{3,2,1,0:T(8,128)S(1)}, f32[1,8,128,128]{3,2,1,0:T(8,128)}, u32[]{:S(2)}) copy-start(f32[1,8,128,128]{3,2,1,0:T(8,128)} %param.7) | copy-start | bytes 1572868
  4.0 59.1 %all-to-all-start = ((f32[1,4,8,128,128]{4,3,1,0,2:T(8,128)}), f32[1,4,8,128,128]{4,3,1,0,2:T(8,128)S(1)}, u32[]{:S(2)}, u32[]{:S(2)}) async-start(f32[1,4,8,128,128]{4,3,1,0,2:T(8,128)} %copy.9), calls=%async_computation | async-start | bytes 4194304 | tf_op jit(solution)/shard_map/gather_terms/all_to_all | solution.py:277
  14.0 37.7 %copy-start.1 = (f32[1,8,128,128]{3,2,1,0:T(8,128)S(1)}, f32[1,8,128,128]{3,2,1,0:T(8,128)}, u32[]{:S(2)}) copy-start(f32[1,8,128,128]{3,2,1,0:T(8,128)} %param.8) | copy-start | bytes 1572868
  14.0 49.1 %copy-start.2 = (s32[1,8]{1,0:T(1,128)S(1)}, s32[1,8]{1,0:T(1,128)}, u32[]{:S(2)}) copy-start(s32[1,8]{1,0:T(1,128)} %kept_ref.3) | copy-start | bytes 100
  49.8 29.9 %collective-permute-start = (f32[2,8,128,128]{3,2,1,0:T(8,128)}, f32[2,8,128,128]{3,2,1,0:T(8,128)}, u32[]{:S(2)}, u32[]{:S(2)}) collective-permute-start(f32[2,8,128,128]{3,2,1,0:T(8,128)} %bitcast.1), channel_id=1, source_target_pairs={{0,8},{8,16},{16,24},{24,32},{32,40},{40,48},{48,56},{56,64},{64,7... | collective-permute-start | bytes 3145736 | tf_op jit(solution)/shard_map/left_previous/ppermute | solution.py:282
  79.7 5.6 %collective-permute-start.1 = (f32[128,128]{1,0:T(8,128)S(1)}, f32[128,128]{1,0:T(8,128)S(1)}, u32[]{:S(2)}, u32[]{:S(2)}) collective-permute-start(f32[128,128]{1,0:T(8,128)S(1)} %get-tuple-element.25), channel_id=1, source_target_pairs={{0,8},{8,16},{16,24},{24,32},{32,40},{40,48},{48,56},{56,64},{64,7... | collective-permute-start | bytes 196616 | tf_op jit(solution)/shard_map/hand_on/ppermute | solution.py:311

commit v6 on v5

--- a/solution.py
+++ b/solution.py
@@ -123,7 +123,7 @@
         sent_ref[target] = sheet
 
 
-def combine_kernel(z_ref, kept_ref, scalars_ref, basis_ref, images_ref, moved_ref, sent_ref):
+def combine_kernel(z_ref, kept_ref, scalars_ref, basis_ref, images_ref, moved_ref, psi_ref):
     sectors, _, size = scalars_ref.shape
     tiny = 1e-30
 
@@ -183,8 +183,7 @@
     result = jnp.where(held, result, 0.0)
     moved = jnp.where(held, moved, 0.0)
     moved_ref[...] = moved
-    for target in range(sectors):
-        sent_ref[target, 0] = result
+    psi_ref[...] = result
 
 
 def fill_kernel(moved_ref, _, sent_ref):
@@ -192,8 +191,10 @@
         sent_ref[target, 1] = moved_ref[...]
 
 
-def stage_kernel(left_ref, out_ref):
+def stage_kernel(left_ref, psi_ref, out_ref, sent_ref):
     own, sectors, _, _ = left_ref.shape
+    for target in range(sectors):
+        sent_ref[target, 0] = psi_ref[...]
     for term in range(own):
         for sector in range(sectors):
             out_ref[term, sector] = left_operand(left_ref[term, sector])
@@ -273,8 +274,8 @@
     spot = z[None]
     pairs = [(source, source + 1) for source in range(63)]
     with jax.named_scope("gather_terms"):
-        outgoing = jnp.concatenate([left, right], axis=0)
-        blocks = lax.all_to_all(outgoing, TERM, 1, 0, axis_index_groups=[list(FIRST)], tiled=False)
+        outgoing = jnp.stack([part[term] for part in (left, right) for term in range(own)], axis=1)
+        blocks = lax.all_to_all(outgoing, TERM, 0, 0, axis_index_groups=[list(FIRST)], tiled=True)
     with jax.named_scope("prefix"):
         prefix = scanned(lax.dynamic_index_in_dim(transfer, z, 0, keepdims=False))
     with jax.named_scope("left_previous"):
@@ -300,21 +301,21 @@
     with jax.named_scope("share_scalars"):
         scalars = lax.all_to_all(sent, TERM, 0, 0, axis_index_groups=[list(FIRST)], tiled=True)
     with jax.named_scope("combine"):
-        moved, sent = call(
+        moved, result = call(
             combine_kernel,
-            (struct(size, size), struct(sectors, 2, size, size)),
+            (struct(size, size), struct(size, size)),
             [smem(), smem()] + [vmem()] * 3,
             size**2 * 100,
         )(spot, kept, scalars, basis, images)
     with jax.named_scope("hand_on"):
         moved, left_previous = lax.optimization_barrier((moved, left_previous))
         moved = lax.ppermute(moved, SITE, pairs)
-        staged = call(
+        staged, sent = call(
             stage_kernel,
-            jax.ShapeDtypeStruct((own, sectors, size, 2 * size), jnp.bfloat16),
-            [vmem()],
+            (jax.ShapeDtypeStruct((own, sectors, size, 2 * size), jnp.bfloat16), struct(sectors, 2, size, size)),
+            [vmem(), vmem()],
             own * sectors * size**3,
-        )(left_previous)
+        )(left_previous, result)
         moved, staged = lax.optimization_barrier((moved, staged))
     with jax.named_scope("share"):
         sent = call(

time: 118 us -> 118 us (level)
    broadcast_in_dim x1 -> x0, other arithmetic: 1.81 us -> none  [per_device(): lax.all_to_all(outgoing, TERM, 1, 0, axis_index_groups=[list(FIRST)], til...]
    squeeze x0 -> x1, local copies, waits for them, and re-layouts: none -> 1.78 us  [per_device(): jnp.stack([part[term] for part in (left, right) for term in range(own)],...]
    broadcast_in_dim x1 -> x0, local copies, waits for them, and re-layouts: 1.58 us -> none  [per_device(): lax.all_to_all(outgoing, TERM, 1, 0, axis_index_groups=[list(FIRST)], til...]
    another operation x0 -> x1, other arithmetic: none -> 1.57 us  [per_device(): jnp.stack([part[term] for part in (left, right) for term in range(own)],...]
where the time goes in v6:
time: 118 us
  blocking collectives  74.9 us (63%)
  starting transfers between devices  13.8 us (12%)
  waiting for transfers between devices  13.3 us (11%)
  Pallas kernels  9.65 us (8%)
  matrix products  2.04 us (2%)
  local copies, waits for them, and re-layouts  1.81 us (2%)
  other arithmetic  1.57 us (1%)
    all_gather x6, blocking collectives, scanned(): pair = lax.all_gather(whole, axis)  33.6 us
    all_to_all x1, blocking collectives, per_device(): lax.all_to_all(sent, TERM, 0, 0, axis_index_groups=[list(LAST)], tiled=True)  30.9 us
    all_to_all x1, waiting for transfers between devices, per_device(): lax.all_to_all(outgoing, TERM, 0, 0, axis_index_groups=[list(FIRST)], til...  11 us
    all_to_all x1, blocking collectives, per_device(): lax.all_to_all(sent, TERM, 0, 0, axis_index_groups=[list(FIRST)], tiled=T...  10.3 us
    all_to_all x1, starting transfers between devices, per_device(): lax.all_to_all(outgoing, TERM, 0, 0, axis_index_groups=[list(FIRST)], til...  9.97 us
    pallas_call x1, Pallas kernels, per_device(): call(krylov_kernel, (struct(ITERS + 1, size, size), struct(ITERS + 1, siz...  4.87 us
  transfers between devices with their start and end apart: 3, of which 2 were waited for; matrix products, arithmetic and copies ran while one was open for 2% of the time, Pallas kernels for 7%

profile of v6, /device:TPU:94, one launch (start us, length us, event | category | flops | bytes accessed | tf_op | source)
XLA Modules:
  0.0 117.8 jit_solution(17913606750790314001)
XLA Ops:
  0.6 0.0 copy-start
  0.6 1.8 %slice_bitcast_fusion.1 = (f32[8,1,128,128]{3,2,1,0:T(8,128)S(1)}, f32[8,1,128,128]{3,2,1,0:T(8,128)S(1)}, f32[8,1,128,128]{3,2,1,0:T(8,128)S(1)}, f32[8,1,128,128]{3,2,1,0:T(8,128)S(1)}) fusion(f32[1,2,8,128,128]{4,3,2,1,0:T(8,128)} %param.6, f32[1,2,8,128,128]{4,3,2,1,0:T(8,128)} %param.5), kind=kLoop, calls=%fused_computation.7 | loop fusion | bytes 4194304 | tf_op jit(solution)/shard_map/gather_terms/stack;gather_terms/squeeze | solution.py:277
  2.4 1.6 %pad_maximum_fusion = f32[8,4,128,128]{3,2,1,0:T(8,128)} fusion(f32[8,1,128,128]{3,2,1,0:T(8,128)S(1)} %get-tuple-element.37, f32[8,1,128,128]{3,2,1,0:T(8,128)S(1)} %get-tuple-element.36, f32[8,1,128,128]{3,2,1,0:T(8,128)S(1)} %get-tuple-element.38, f32[8,1,128,128]{3,2,1,0:T(8,128)S(1)} %get-tuple-element.39), kind=kLoop, calls=%fused_computation | loop fusion | flops 1572864 | bytes 4194304 | tf_op jit(solution)/shard_map/gather_terms/stack | solution.py:277
  4.0 10.0 %all-to-all-start = ((f32[8,4,128,128]{3,2,1,0:T(8,128)}), f32[8,4,128,128]{3,2,1,0:T(8,128)S(1)}, u32[]{:S(2)}, u32[]{:S(2)}) async-start(f32[8,4,128,128]{3,2,1,0:T(8,128)} %pad_maximum_fusion), calls=%async_computation | async-start | bytes 4194304 | tf_op jit(solution)/shard_map/gather_terms/all_to_all | solution.py:278
  14.0 0.0 copy-start.1
  14.0 0.0 copy-start.2
  14.0 0.0 copy-done
  14.0 2.0 %all-gather = f32[2,1,128,128]{3,2,1,0:T(8,128)S(1)} all-gather(f32[1,1,128,128]{3,2,1,0:T(8,128)S(1)} %constant_dynamic-slice_fusion), channel_id=2, replica_groups=mesh['y2'=2,'y1'=2,'y0'=2,'x1'=2,'x0'=2,'c'=2,'z'=8] {'c'}, dimensions={0}, use_global_device_ids=true | all-gather | bytes 196608 | tf_op jit(solution)/shard_map/prefix/scan_c/all_gather | solution.py:258
  16.0 0.2 fusion.9
  16.2 4.9 %all-gather.1 = f32[256,128]{1,0:T(8,128)S(1)} all-gather(f32[128,128]{1,0:T(8,128)S(1)} %fusion.9), channel_id=3, replica_groups=mesh['y2'=2,'y1'=2,'y0'=2,'x1'=2,'x0'=2,'c'=2,'z'=8] {'x0'}, dimensions={0}, use_global_device_ids=true | all-gather | bytes 196608 | tf_op jit(solution)/shard_map/prefix/scan_x0/all_gather | solution.py:258
  21.2 0.2 fusion.7
  21.4 6.4 %all-gather.2 = f32[256,128]{1,0:T(8,128)S(1)} all-gather(f32[128,128]{1,0:T(8,128)S(1)} %fusion.7), channel_id=4, replica_groups=mesh['y2'=2,'y1'=2,'y0'=2,'x1'=2,'x0'=2,'c'=2,'z'=8] {'x1'}, dimensions={0}, use_global_device_ids=true | all-gather | bytes 196608 | tf_op jit(solution)/shard_map/prefix/scan_x1/all_gather | solution.py:258
  27.8 0.2 fusion.5
  28.1 4.9 %all-gather.3 = f32[256,128]{1,0:T(8,128)S(1)} all-gather(f32[128,128]{1,0:T(8,128)S(1)} %fusion.5), channel_id=5, replica_groups=mesh['y2'=2,'y1'=2,'y0'=2,'x1'=2,'x0'=2,'c'=2,'z'=8] {'y0'}, dimensions={0}, use_global_device_ids=true | all-gather | bytes 196608 | tf_op jit(solution)/shard_map/prefix/scan_y0/all_gather | solution.py:258
  33.0 0.2 fusion.3
  33.2 6.4 %all-gather.4 = f32[256,128]{1,0:T(8,128)S(1)} all-gather(f32[128,128]{1,0:T(8,128)S(1)} %fusion.3), channel_id=6, replica_groups=mesh['y2'=2,'y1'=2,'y0'=2,'x1'=2,'x0'=2,'c'=2,'z'=8] {'y1'}, dimensions={0}, use_global_device_ids=true | all-gather | bytes 196608 | tf_op jit(solution)/shard_map/prefix/scan_y1/all_gather | solution.py:258
  39.6 0.2 fusion.1
  39.8 8.8 %all-gather.5 = f32[256,128]{1,0:T(8,128)S(1)} all-gather(f32[128,128]{1,0:T(8,128)S(1)} %fusion.1), channel_id=7, replica_groups=mesh['y2'=2,'y1'=2,'y0'=2,'x1'=2,'x0'=2,'c'=2,'z'=8] {'y2'}, dimensions={0}, use_global_device_ids=true | all-gather | bytes 196608 | tf_op jit(solution)/shard_map/prefix/scan_y2/all_gather | solution.py:258
  48.7 0.2 convolution_select_fusion.4
  48.9 0.2 convolution_select_fusion.3
  49.1 0.2 convolution_select_fusion.2
  49.3 0.2 convolution_select_fusion.1
  49.6 0.2 convolution_select_fusion.prefix_ref
  49.8 1.9 %collective-permute-start = (f32[2,8,128,128]{3,2,1,0:T(8,128)}, f32[2,8,128,128]{3,2,1,0:T(8,128)}, u32[]{:S(2)}, u32[]{:S(2)}) collective-permute-start(f32[2,8,128,128]{3,2,1,0:T(8,128)} %bitcast.10), channel_id=1, source_target_pairs={{0,8},{8,16},{16,24},{24,32},{32,40},{40,48},{48,56},{56,64},{64,7... | collective-permute-start | bytes 3145736 | tf_op jit(solution)/shard_map/left_previous/ppermute | solution.py:283
  51.7 0.0 copy-done.1
  51.7 0.3 prepare.1
  52.1 11.0 %all-to-all-done.blocks_ref = f32[8,4,128,128]{3,2,1,0:T(8,128)S(1)} async-done(((f32[8,4,128,128]{3,2,1,0:T(8,128)}), f32[8,4,128,128]{3,2,1,0:T(8,128)S(1)}, u32[]{:S(2)}, u32[]{:S(2)}) %all-to-all-start) | async-done | bytes 2097184 | tf_op jit(solution)/shard_map/gather_terms/all_to_all | solution.py:278
  63.1 0.0 copy-done.2
  63.1 4.9 %krylov.1 = (f32[5,128,128]{2,1,0:T(8,128)S(1)}, f32[5,128,128]{2,1,0:T(8,128)S(1)}, f32[8,8,128]{2,1,0:T(8,128)S(1)}) custom-call(s32[1]{0:T(128)} %bitcast.z_ref, s32[1,8]{1,0:T(1,128)S(1)} %copy-done.2, f32[8,4,128,128]{3,2,1,0:T(8,128)S(1)} %all-to-all-done.blocks_ref, f32[128,128]{1,0:T(8,128)S(1)} %get-tuple-element.18.x_ref, ...), custom_call_target="tpu_custom_call" | custom-call | flops 3221225472 | bytes 4194304 | tf_op jit(solution)/shard_map/krylov/pallas_call | solution.py:294
  67.9 10.3 %all_to_all.15.scalars_ref = f32[8,8,128]{2,1,0:T(8,128)S(1)} all-to-all(f32[8,8,128]{2,1,0:T(8,128)S(1)} %get-tuple-element.22), channel_id=1, replica_groups={{0,4,1,5,2,6,3,7},{8,12,9,13,10,14,11,15},{16,20,17,21,18,22,19,23},{24..., dimensions={0} | all-to-all | bytes 65536 | tf_op jit(solution)/shard_map/share_scalars/all_to_all | solution.py:302
  78.3 1.3 %combine.1 = (f32[128,128]{1,0:T(8,128)S(1)}, f32[128,128]{1,0:T(8,128)S(1)}) custom-call(s32[1]{0:T(128)} %bitcast.z_ref, s32[1,8]{1,0:T(1,128)S(1)} %copy-done.2, f32[8,8,128]{2,1,0:T(8,128)S(1)} %all_to_all.15.scalars_ref, f32[5,128,128]{2,1,0:T(8,128)S(1)} %get-tuple-element.23.basis_ref, f32[5,128,128]{2,1,0:T(8,128)S(1)} %get-tuple-element.24.images_ref), custom_call_target="tpu_custom_call" | custom-call | flops 1638400 | bytes 4194304 | tf_op jit(solution)/shard_map/combine/pallas_call | solution.py:304
  79.6 0.0 collective-permute-done.left_ref
  79.6 1.9 %collective-permute-start.1 = (f32[128,128]{1,0:T(8,128)S(1)}, f32[128,128]{1,0:T(8,128)S(1)}, u32[]{:S(2)}, u32[]{:S(2)}) collective-permute-start(f32[128,128]{1,0:T(8,128)S(1)} %get-tuple-element.27), channel_id=1, source_target_pairs={{0,8},{8,16},{16,24},{24,32},{32,40},{40,48},{48,56},{56,64},{64,7... | collective-permute-start | bytes 196616 | tf_op jit(solution)/shard_map/hand_on/ppermute | solution.py:312
  81.5 1.4 %hand_on.1 = (bf16[2,8,128,256]{3,2,1,0:T(8,128)(2,1)S(1)}, f32[8,2,128,128]{3,2,1,0:T(8,128)S(1)}) custom-call(f32[2,8,128,128]{3,2,1,0:T(8,128)} %collective-permute-done.left_ref, f32[128,128]{1,0:T(8,128)S(1)} %get-tuple-element.29.psi_ref), custom_call_target="tpu_custom_call" | custom-call | flops 33554432 | bytes 4194304 | tf_op jit(solution)/shard_map/hand_on/pallas_call | solution.py:313
  82.9 2.3 %collective-permute-done.1.moved_ref = f32[128,128]{1,0:T(8,128)S(1)} collective-permute-done((f32[128,128]{1,0:T(8,128)S(1)}, f32[128,128]{1,0:T(8,128)S(1)}, u32[]{:S(2)}, u32[]{:S(2)}) %collective-permute-start.1) | collective-permute-done | bytes 65568 | tf_op jit(solution)/shard_map/hand_on/ppermute | solution.py:312
  85.2 30.9 %all_to_all.16.shared_ref = f32[8,2,128,128]{3,2,1,0:T(8,128)S(1)} all-to-all(f32[8,2,128,128]{3,2,1,0:T(8,128)S(1)} %share.1), channel_id=1, replica_groups={{7,6,5,4,3,2,1,0},{15,14,13,12,11,10,9,8},{23,22,21,20,19,18,17,16},{31..., dimensions={0} | all-to-all | bytes 2097152 | tf_op jit(solution)/shard_map/share/all_to_all | solution.py:328
  116.1 1.7 %boundary.1 = (f32[1,8,128,128]{3,2,1,0:T(8,128)}, f32[1,2,8,128,128]{4,3,2,1,0:T(8,128)}) custom-call(f32[8,2,128,128]{3,2,1,0:T(8,128)S(1)} %all_to_all.16.shared_ref, bf16[2,8,128,256]{3,2,1,0:T(8,128)(2,1)S(1)} %get-tuple-element.33.left_ref), custom_call_target="tpu_custom_call" | custom-call | flops 402653184 | bytes 4194304 | tf_op jit(solution)/shard_map/boundary/pallas_call | solution.py:330
  (2 shorter events, 0.0 us)
Async XLA Ops:
  0.6 13.3 %copy-start = (f32[1,8,128,128]{3,2,1,0:T(8,128)S(1)}, f32[1,8,128,128]{3,2,1,0:T(8,128)}, u32[]{:S(2)}) copy-start(f32[1,8,128,128]{3,2,1,0:T(8,128)} %param.7) | copy-start | bytes 1572868
  4.0 59.1 %all-to-all-start = ((f32[8,4,128,128]{3,2,1,0:T(8,128)}), f32[8,4,128,128]{3,2,1,0:T(8,128)S(1)}, u32[]{:S(2)}, u32[]{:S(2)}) async-start(f32[8,4,128,128]{3,2,1,0:T(8,128)} %pad_maximum_fusion), calls=%async_computation | async-start | bytes 4194304 | tf_op jit(solution)/shard_map/gather_terms/all_to_all | solution.py:278
  14.0 37.7 %copy-start.1 = (f32[1,8,128,128]{3,2,1,0:T(8,128)S(1)}, f32[1,8,128,128]{3,2,1,0:T(8,128)}, u32[]{:S(2)}) copy-start(f32[1,8,128,128]{3,2,1,0:T(8,128)} %param.8) | copy-start | bytes 1572868
  14.0 49.1 %copy-start.2 = (s32[1,8]{1,0:T(1,128)S(1)}, s32[1,8]{1,0:T(1,128)}, u32[]{:S(2)}) copy-start(s32[1,8]{1,0:T(1,128)} %kept_ref.3) | copy-start | bytes 100
  49.8 29.8 %collective-permute-start = (f32[2,8,128,128]{3,2,1,0:T(8,128)}, f32[2,8,128,128]{3,2,1,0:T(8,128)}, u32[]{:S(2)}, u32[]{:S(2)}) collective-permute-start(f32[2,8,128,128]{3,2,1,0:T(8,128)} %bitcast.10), channel_id=1, source_target_pairs={{0,8},{8,16},{16,24},{24,32},{32,40},{40,48},{48,56},{56,64},{64,7... | collective-permute-start | bytes 3145736 | tf_op jit(solution)/shard_map/left_previous/ppermute | solution.py:283
  79.6 5.6 %collective-permute-start.1 = (f32[128,128]{1,0:T(8,128)S(1)}, f32[128,128]{1,0:T(8,128)S(1)}, u32[]{:S(2)}, u32[]{:S(2)}) collective-permute-start(f32[128,128]{1,0:T(8,128)S(1)} %get-tuple-element.27), channel_id=1, source_target_pairs={{0,8},{8,16},{16,24},{24,32},{32,40},{40,48},{48,56},{56,64},{64,7... | collective-permute-start | bytes 196616 | tf_op jit(solution)/shard_map/hand_on/ppermute | solution.py:312
